TPU v7x, 32 devices: a whole 2x2x4 slice. The times are simulated.
32 devices in a mesh: section: 4 (over y, x), tile: 8 (over z, core).
Axes of the slice: x: 2, y: 2, z: 4, core: 2. Of those that a mesh axis runs over, the one named last changes fastest.
Arguments:
- activations: bfloat16 [8, 8, 16, 16, 256], P('section', 'tile'), may hold values from -6 to 6
- weight: bfloat16 [4, 9, 256, 256], P('section'), may hold values from -0.125 to 0.125
- conv_bias: bfloat16 [4, 256], P('section'), may hold values from -3 to 3
- norm_gain: bfloat16 [4, 256], P('section'), may hold values from 0.099609375 to 1.8984375
- metric: bfloat16 [8, 9, 256], P('tile'), may hold values from 0.5 to 2
- neighbours: int32 [3, 8, 8], replicated, may hold values from 0 to 7, as said below
Outputs:
- advanced: bfloat16 [8, 8, 16, 16, 256], P('section', 'tile')
Inputs may be any that keep to these rules, and one draw needn't show every extreme that they name: `neighbours`: row 0 names neighbour tiles; each of the 8 columns names every tile once. Row 1 is a side or corner number 0 to 3. Row 2 is 0 or 1 for the 4 side columns and 0 for the corner columns.
All inputs are finite; a program needn't handle non-finite values.
Results may differ from a plain program's by a relative error of at most 0.0075.
Values may be sent and summed in bfloat16 or wider, within the bound.
No kernel may reach another device: no remote copies, remote signals or barrier semaphores. Data moves between devices by JAX's collectives and lax.ppermute only.
A program may use at most 64 MiB of HBM per device.

v0:
```python
import jax
import jax.numpy as jnp
from jax import lax
from jax.sharding import PartitionSpec as P


def shifted_2(value, axis, by):
    peers = lax.axis_size(axis)
    return lax.ppermute(value, axis, [(i, (i + by) % peers) for i in range(peers)])


def normalize(states, gain_row):
    values = states.astype(jnp.float32)
    mean_sq = jnp.mean(values * values, axis=-1, keepdims=True)
    return (values * lax.rsqrt(mean_sq + 1e-05) * gain_row.astype(jnp.float32)).astype(jnp.bfloat16)


def side_strips(normed):
    side_len = normed.shape[1]
    return jnp.stack(
        [normed[:, 0], normed[:, :, side_len - 1], normed[:, side_len - 1], normed[:, :, 0]], axis=1
    )


def assemble(normed, strips, corners):
    top_row = jnp.concatenate([corners[0][:, None], strips[0], corners[1][:, None]], axis=1)
    middle = jnp.concatenate([strips[3][:, :, None], normed, strips[1][:, :, None]], axis=2)
    bottom = jnp.concatenate([corners[3][:, None], strips[2], corners[2][:, None]], axis=1)
    return jnp.concatenate([top_row[:, None], middle, bottom[:, None]], axis=1)


def convolve(padded, weight_taps, metric_taps, side_len):
    count = padded.shape[0]
    channels = padded.shape[-1]
    total = jnp.zeros((count, side_len * side_len, channels), jnp.float32)
    for row_off in range(3):
        for col_off in range(3):
            tap_index = row_off * 3 + col_off
            shifted = padded[
                :, row_off : row_off + side_len, col_off : col_off + side_len, :
            ].reshape(-1, channels)
            product = jnp.dot(shifted, weight_taps[tap_index], preferred_element_type=jnp.float32)
            product = product.reshape(count, side_len * side_len, channels)
            total = total + product * metric_taps[:, tap_index, :, None].astype(jnp.float32)
    return total


def advance(micro_batch, weight_taps, bias_row, gain_row, metric_own, own_lists):
    states = micro_batch[:, 0]
    side_len = states.shape[1]
    normed = normalize(states, gain_row)
    borders = side_strips(normed)
    gathered = lax.all_gather(borders[:, None], "tile", axis=1, tiled=True)
    strips = []
    for side_index in range(4):
        source = own_lists[0, side_index]
        which = own_lists[1, side_index]
        strip_rows = gathered[:, source, which]
        strip_rows = jnp.where(own_lists[2, side_index] == 1, strip_rows[:, ::-1], strip_rows)
        strips.append(strip_rows)
    corners = []
    for corner_index in range(4):
        source = own_lists[0, 4 + corner_index]
        which = own_lists[1, 4 + corner_index]
        rim_index = jnp.where(which < 2, 0, 2)
        position = jnp.where((which == 1) | (which == 2), side_len - 1, 0)
        corners.append(gathered[:, source, rim_index, position])
    padded = assemble(normed, strips, corners)
    conv = convolve(padded, weight_taps, metric_own, side_len)
    conv = conv.reshape(states.shape)
    result = states.astype(jnp.float32) + jax.nn.silu(conv + bias_row.astype(jnp.float32))
    return result.astype(jnp.bfloat16)[:, None]


def local(activations, weight, conv_bias, norm_gain, metric, neighbours):
    tile_id = lax.axis_index("tile")
    own_lists = lax.dynamic_index_in_dim(neighbours, tile_id, axis=1, keepdims=False)
    sections = lax.axis_size("section")
    current = activations
    for section_step in range(sections):
        current = advance(current, weight[0], conv_bias[0], norm_gain[0], metric, own_lists)
        current = shifted_2(current, "section", 1)
    return current


def solution(mesh):
    in_specs = (
        P("section", "tile", None, None, None),
        P("section", None, None, None),
        P("section", None),
        P("section", None),
        P("tile", None, None),
        P(),
    )
    out_specs = P("section", "tile", None, None, None)
    return jax.shard_map(local, mesh=mesh, in_specs=in_specs, out_specs=out_specs, check_vma=False)
```

profile of v0, /device:TPU:0, one launch (start us, length us, event | category | flops | bytes accessed | tf_op | source)
XLA Modules:
  0.0 157.3 jit_solution(7260312293615303172)
XLA Ops:
  0.0 0.7 convert_element_type.343
  0.7 1.1 fusion.49
  1.9 1.1 fusion.51
  3.1 0.7 fusion.161
  13.0 0.6 slice.417
  27.1 16.6 %all-gather = bf16[2,32,16,256]{3,2,0,1:T(8,128)(2,1)S(1)} all-gather(bf16[2,4,16,256]{3,2,0,1:T(8,128)(2,1)S(1)} %pad_maximum_fusion.12), channel_id=2, replica_groups=mesh['section'=4,'tile'=8] {'tile'}, dimensions={1}, use_global_device_ids=true | all-gather | bytes 589824 | tf_op jit(solution)/shard_map/all_gather | solution.py:53
  54.1 0.2 pad_maximum_fusion.10
  54.4 0.4 pad_maximum_fusion
  55.0 0.5 copy-done.3
  55.9 0.6 copy-done.4
  56.5 0.6 copy-done.1
  57.5 0.2 fusion.30
  58.5 0.2 fusion.26
  59.4 1.5 collective-permute-start
  60.9 8.0 %collective-permute-done = bf16[2,1,16,16,256]{4,3,0,2,1:T(8,128)(2,1)S(1)} collective-permute-done((bf16[2,1,16,16,256]{4,3,0,2,1:T(8,128)(2,1)S(1)}, bf16[2,1,16,16,256]{4,3,0,2,1:T(8,128)(2,1)S(1)}, u32[]{:S(2)}, u32[]{:S(2)}) %collective-permute-start) | collective-permute-done | bytes 262176 | tf_op jit(solution)/shard_map/ppermute | solution.py:9
  69.4 14.8 %all-gather.1 = bf16[2,32,16,256]{3,2,0,1:T(8,128)(2,1)S(1)} all-gather(bf16[2,4,16,256]{3,2,0,1:T(8,128)(2,1)S(1)} %pad_maximum_fusion.13), channel_id=3, replica_groups=mesh['section'=4,'tile'=8] {'tile'}, dimensions={1}, use_global_device_ids=true | all-gather | bytes 589824 | tf_op jit(solution)/shard_map/all_gather | solution.py:53
  84.8 0.2 pad_maximum_fusion.8
  85.1 0.4 pad_maximum_fusion.1
  87.1 0.2 fusion.20
  88.5 0.6 collective-permute-start.1
  89.1 8.9 %collective-permute-done.1 = bf16[2,1,16,16,256]{4,3,0,2,1:T(8,128)(2,1)S(1)} collective-permute-done((bf16[2,1,16,16,256]{4,3,0,2,1:T(8,128)(2,1)S(1)}, bf16[2,1,16,16,256]{4,3,0,2,1:T(8,128)(2,1)S(1)}, u32[]{:S(2)}, u32[]{:S(2)}) %collective-permute-start.1) | collective-permute-done | bytes 262176 | tf_op jit(solution)/shard_map/ppermute | solution.py:9
  98.4 15.1 %all-gather.2 = bf16[2,32,16,256]{3,2,0,1:T(8,128)(2,1)S(1)} all-gather(bf16[2,4,16,256]{3,2,0,1:T(8,128)(2,1)S(1)} %pad_maximum_fusion.14), channel_id=4, replica_groups=mesh['section'=4,'tile'=8] {'tile'}, dimensions={1}, use_global_device_ids=true | all-gather | bytes 589824 | tf_op jit(solution)/shard_map/all_gather | solution.py:53
  114.1 0.2 pad_maximum_fusion.6
  114.4 0.4 pad_maximum_fusion.2
  117.9 9.4 %collective-permute-done.2 = bf16[2,1,16,16,256]{4,3,0,2,1:T(8,128)(2,1)S(1)} collective-permute-done((bf16[2,1,16,16,256]{4,3,0,2,1:T(8,128)(2,1)S(1)}, bf16[2,1,16,16,256]{4,3,0,2,1:T(8,128)(2,1)S(1)}, u32[]{:S(2)}, u32[]{:S(2)}) %collective-permute-start.2) | collective-permute-done | bytes 262176 | tf_op jit(solution)/shard_map/ppermute | solution.py:9
  127.8 15.0 %all-gather.3 = bf16[2,32,16,256]{3,2,0,1:T(8,128)(2,1)S(1)} all-gather(bf16[2,4,16,256]{3,2,0,1:T(8,128)(2,1)S(1)} %pad_maximum_fusion.15), channel_id=5, replica_groups=mesh['section'=4,'tile'=8] {'tile'}, dimensions={1}, use_global_device_ids=true | all-gather | bytes 589824 | tf_op jit(solution)/shard_map/all_gather | solution.py:53
  143.4 0.2 pad_maximum_fusion.4
  143.7 0.4 pad_maximum_fusion.3
  145.7 0.2 fusion.4
  146.7 0.2 fusion
  147.2 9.4 %collective-permute-done.3 = bf16[2,1,16,16,256]{4,3,0,2,1:T(8,128)(2,1)S(1)} collective-permute-done((bf16[2,1,16,16,256]{4,3,0,2,1:T(8,128)(2,1)S(1)}, bf16[2,1,16,16,256]{4,3,0,2,1:T(8,128)(2,1)S(1)}, u32[]{:S(2)}, u32[]{:S(2)}) %collective-permute-start.3) | collective-permute-done | bytes 262176 | tf_op jit(solution)/shard_map/ppermute | solution.py:9
  156.6 0.7 copy.533
  (195 shorter events, 13.9 us)
Async XLA Ops:
  0.0 3.0 %copy-start = (s32[3,8,8]{2,1,0:T(8,128)S(1)}, s32[3,8,8]{2,1,0:T(8,128)}, u32[]{:S(2)}) copy-start(s32[3,8,8]{2,1,0:T(8,128)} %param.11) | copy-start | bytes 2308
  0.0 26.9 %copy-start.2 = (bf16[2,1,16,16,256]{4,3,2,1,0:T(8,128)(2,1)S(1)}, bf16[2,1,16,16,256]{4,3,2,1,0:T(8,128)(2,1)}, u32[]{:S(2)}) copy-start(bf16[2,1,16,16,256]{4,3,2,1,0:T(8,128)(2,1)} %param.6) | copy-start | bytes 786436
  54.8 0.7 copy-start.3
  55.8 0.7 copy-start.4
  55.8 1.3 copy-start.1
  59.4 9.5 %collective-permute-start = (bf16[2,1,16,16,256]{4,3,0,2,1:T(8,128)(2,1)S(1)}, bf16[2,1,16,16,256]{4,3,0,2,1:T(8,128)(2,1)S(1)}, u32[]{:S(2)}, u32[]{:S(2)}) collective-permute-start(bf16[2,1,16,16,256]{4,3,0,2,1:T(8,128)(2,1)S(1)} %fusion.54), channel_id=1, source_target_pairs={{0,8},{8,16},{16,24},{24,0},{1,9},{9,17},{17,25},{25,1},{2,10},{10... | collective-permute-start | bytes 786440 | tf_op jit(solution)/shard_map/ppermute | solution.py:9
  88.5 9.5 %collective-permute-start.1 = (bf16[2,1,16,16,256]{4,3,0,2,1:T(8,128)(2,1)S(1)}, bf16[2,1,16,16,256]{4,3,0,2,1:T(8,128)(2,1)S(1)}, u32[]{:S(2)}, u32[]{:S(2)}) collective-permute-start(bf16[2,1,16,16,256]{4,3,0,2,1:T(8,128)(2,1)S(1)} %fusion.57), channel_id=1, source_target_pairs={{0,8},{8,16},{16,24},{24,0},{1,9},{9,17},{17,25},{25,1},{2,10},{10... | collective-permute-start | bytes 786440 | tf_op jit(solution)/shard_map/ppermute | solution.py:9
  117.8 9.5 %collective-permute-start.2 = (bf16[2,1,16,16,256]{4,3,0,2,1:T(8,128)(2,1)S(1)}, bf16[2,1,16,16,256]{4,3,0,2,1:T(8,128)(2,1)S(1)}, u32[]{:S(2)}, u32[]{:S(2)}) collective-permute-start(bf16[2,1,16,16,256]{4,3,0,2,1:T(8,128)(2,1)S(1)} %fusion.60), channel_id=1, source_target_pairs={{0,8},{8,16},{16,24},{24,0},{1,9},{9,17},{17,25},{25,1},{2,10},{10... | collective-permute-start | bytes 786440 | tf_op jit(solution)/shard_map/ppermute | solution.py:9
  147.1 9.5 %collective-permute-start.3 = (bf16[2,1,16,16,256]{4,3,0,2,1:T(8,128)(2,1)S(1)}, bf16[2,1,16,16,256]{4,3,0,2,1:T(8,128)(2,1)S(1)}, u32[]{:S(2)}, u32[]{:S(2)}) collective-permute-start(bf16[2,1,16,16,256]{4,3,0,2,1:T(8,128)(2,1)S(1)} %fusion.63), channel_id=1, source_target_pairs={{0,8},{8,16},{16,24},{24,0},{1,9},{9,17},{17,25},{25,1},{2,10},{10... | collective-permute-start | bytes 786440 | tf_op jit(solution)/shard_map/ppermute | solution.py:9
where the time goes:
time: 158 us; the launch traced here: 157 us
  blocking collectives  61.5 us (39%)
  waiting for transfers between devices  35.7 us (23%)
  between operations  33.8 us (21%)
  matrix products  8.28 us (5%)
  local copies, waits for them, and re-layouts  7.89 us (5%)
  other arithmetic  7.84 us (5%)
  starting transfers between devices  2.31 us (1%)
    all_gather x4, blocking collectives, advance(): gathered = lax.all_gather(borders[:, None], 'tile', axis=1, tiled=True)  61.5 us
    ppermute x4, waiting for transfers between devices, shifted_2(): lax.ppermute(value, axis, [(i, (i + by) % peers) for i in range(peers)])  35.7 us
    dot_general x36, matrix products, convolve(): jnp.dot(shifted, weight_taps[tap_index], preferred_element_type=jnp.float32)  8.28 us
  transfers between devices with their start and end apart: 4, of which 4 were waited for; matrix products, arithmetic and copies ran while one was open for 0% of the time, Pallas kernels for 0%

commit v1 on v0

v1 whole, which is shorter than its diff:
```python
import functools

import jax
import jax.numpy as jnp
from jax import lax
from jax.experimental import pallas as pl
from jax.experimental.pallas import tpu as pltpu
from jax.sharding import PartitionSpec as P

BF16 = jnp.bfloat16
F32 = jnp.float32
EXTRA = 16


def swap(value, axis, by):
    peers = lax.axis_size(axis)
    return lax.ppermute(value, axis, [(i, i ^ by) for i in range(peers)])


def fetch(value, axis, by):
    peers = lax.axis_size(axis)
    return lax.ppermute(value, axis, [((i + by) % peers, i) for i in range(peers)])


def layer_kernel(side, tiles, outs, first, last, *refs):
    ids, near = refs[0], refs[1]
    refs = refs[2:]
    if first:
        even, odd, w, par, out = refs[:5]
        refs = refs[5:]
    else:
        even, odd, states, half_a, half_b, out = refs[:6]
        w, par, sem = refs[6:9]
        refs = refs[9:]
    center, pick, strips, pads, x = refs
    px = side * side
    ch = center.shape[-1]
    own = ids[0]
    core = ids[1]

    if not first:
        rows = half_a.shape[0] - EXTRA
        at_a = pl.multiple_of(core * rows, 128)
        at_b = pl.multiple_of((1 - core) * rows, 128)
        copies = [
            pltpu.make_async_copy(half_a.at[pl.ds(0, rows)], w.at[pl.ds(at_a, rows)], sem.at[0]),
            pltpu.make_async_copy(half_b.at[pl.ds(0, rows)], w.at[pl.ds(at_b, rows)], sem.at[1]),
            pltpu.make_async_copy(half_a.at[pl.ds(rows, EXTRA)], par, sem.at[2]),
        ]
        for copy in copies:
            copy.start()
        copies[2].wait()

    params = par[...].astype(F32)
    gain = params[0:1]
    bias = params[1:2]

    def load(j, odd_one):
        if first:
            return (odd if odd_one else even)[j, 0:px, :]
        return states[2 * j + odd_one]

    strip_rows = lax.broadcasted_iota(jnp.int32, (8 * side, px), 0)
    pixel = lax.broadcasted_iota(jnp.int32, (8 * side, px), 1)
    which = (strip_rows // side) % 4
    place = strip_rows % side
    place = jnp.where(strip_rows // side >= 4, side - 1 - place, place)
    wanted = jnp.where(
        which == 0,
        place,
        jnp.where(which == 1, place * side + side - 1, jnp.where(which == 2, px - side + place, place * side)),
    )
    pick[...] = jnp.where(pixel == wanted, 1.0, 0.0).astype(BF16)

    def prepare(j, odd_one):
        b = 2 * j + odd_one
        v = load(j, odd_one).astype(F32)
        mean_sq = jnp.mean(v * v, axis=-1, keepdims=True)
        z = (v * lax.rsqrt(mean_sq + 1e-05) * gain).astype(BF16)
        center[b] = z
        rims = jnp.dot(pick[...], z, preferred_element_type=F32)
        strips[b] = rims.reshape(8, side, ch)

    @pl.loop(0, tiles // 2)
    def _(j):
        prepare(j, 0)
        prepare(j, 1)

    if not first:
        copies[0].wait()
        copies[1].wait()

    col = lax.broadcasted_iota(jnp.int32, (side + 2, side, ch), 1)

    def build(b, j, odd_one, place):
        tile = own ^ b
        frame = []
        for s in range(4):
            frame.append(strips[own ^ near[0, tile, s], 4 * near[2, tile, s] + near[1, tile, s]])
        corner = []
        for k in range(4):
            which = near[1, tile, 4 + k]
            far = ((which == 1) | (which == 2)).astype(jnp.int32)
            rim_at = jnp.where(which < 2, 0, 2)
            corner.append(strips[own ^ near[0, tile, 4 + k], 4 * far + rim_at, 0:1])
        rows = center[b].astype(F32).reshape(side, side, ch)
        full = jnp.concatenate([frame[0][None], rows, frame[2][None]], axis=0)
        left = jnp.concatenate([corner[0], frame[3], corner[3]], axis=0)
        right = jnp.concatenate([corner[1], frame[1], corner[2]], axis=0)
        shape = (side + 2, side, ch)
        before = jnp.where(col == 0, jnp.broadcast_to(left[:, None, :], shape), pltpu.roll(full, 1, 1))
        after = jnp.where(col == side - 1, jnp.broadcast_to(right[:, None, :], shape), pltpu.roll(full, side - 1, 1))
        pads[0] = before.astype(BF16)
        pads[1] = full.astype(BF16)
        pads[2] = after.astype(BF16)
        metric = (odd if odd_one else even)[j, px : px + EXTRA, :].astype(F32)
        metric = jnp.transpose(metric)
        for q in range(9):
            a, c = q // 3, q % 3
            scale = jnp.broadcast_to(metric[:, q : q + 1], (px, ch)).astype(BF16)
            x[place * px : (place + 1) * px, q * ch : (q + 1) * ch] = pads[c, a : a + side].reshape(px, ch) * scale

    def finish(conv, j, odd_one, slot):
        u = conv + bias
        v = load(j, odd_one).astype(F32)
        out[slot] = (v + u / (1.0 + jnp.exp(-u))).astype(BF16)

    if last:
        build(0, 0, 0, 0)
        build(2, 1, 0, 1)
        conv = jnp.dot(x[...], w[...], preferred_element_type=F32)
        finish(conv[:px], 0, 0, 0)
        finish(conv[px:], 1, 0, 1)
    else:

        @pl.loop(0, tiles // 2)
        def _(j):
            build(2 * j, j, 0, 0)
            build(2 * j + 1, j, 1, 1)
            conv = jnp.dot(x[...], w[...], preferred_element_type=F32)
            finish(conv[:px], j, 0, 2 * j)
            finish(conv[px:], j, 1, 2 * j + 1)


def layer(first, last, ids, near, even, odd, states, weights):
    half = even.shape[0]
    tiles = 2 * half
    ch = even.shape[-1]
    px = even.shape[1] - EXTRA
    side = int(px**0.5)
    outs = 2 if last else tiles
    vmem = pl.BlockSpec(memory_space=pltpu.VMEM)
    smem = pl.BlockSpec(memory_space=pltpu.SMEM)
    hbm = pl.BlockSpec(memory_space=pl.ANY)
    scratch = [
        pltpu.VMEM((tiles, px, ch), BF16),
        pltpu.VMEM((8 * side, px), BF16),
        pltpu.VMEM((tiles, 8, side, ch), F32),
        pltpu.VMEM((3, side + 2, side, ch), BF16),
        pltpu.VMEM((2 * px, 9 * ch), BF16),
    ]
    if first:
        args = [ids, near, even, odd, *weights]
        specs = [smem, smem, vmem, vmem, vmem, vmem]
    else:
        args = [ids, near, even, odd, states, *weights]
        specs = [smem, smem, vmem, vmem, vmem, hbm, hbm]
        scratch = [pltpu.VMEM((9 * ch, ch), BF16), pltpu.VMEM((EXTRA, ch), BF16), pltpu.SemaphoreType.DMA((3,))] + scratch
    rows = outs * px
    return pl.pallas_call(
        functools.partial(layer_kernel, side, tiles, outs, first, last),
        out_shape=jax.ShapeDtypeStruct((outs, px, ch), BF16),
        in_specs=specs,
        out_specs=vmem,
        scratch_shapes=scratch,
        compiler_params=pltpu.CompilerParams(vmem_limit_bytes=48 * 2**20),
        cost_estimate=pl.CostEstimate(flops=2 * rows * 9 * ch * ch, bytes_accessed=4 * rows * ch, transcendentals=rows * ch),
    )(*args)


def local(activations, weight, conv_bias, norm_gain, metric, neighbours):
    sections = lax.axis_size("section")
    tiles = lax.axis_size("tile")
    own = lax.axis_index("tile")
    core = own & 1
    group = (own >> 1) & 1
    side, ch = activations.shape[2], activations.shape[-1]
    px = side * side
    ids = jnp.stack([own, core]).astype(jnp.int32)

    params = jnp.concatenate([norm_gain, conv_bias, jnp.zeros((EXTRA - 2, ch), BF16)], axis=0)
    flat = weight.reshape(-1, ch)
    rows = flat.shape[0] // 2
    half = jnp.concatenate([lax.dynamic_slice_in_dim(flat, core * rows, rows, 0), params], axis=0)
    halves = [fetch(half, "section", k) for k in range(1, sections)]

    extra = jnp.concatenate([metric[0].reshape(9, px), jnp.zeros((EXTRA - 9, px), BF16)], axis=0)
    batches = activations.reshape(2, px, ch)
    mine = jnp.concatenate([lax.dynamic_index_in_dim(batches, group, 0, False), extra], axis=0)
    other = jnp.concatenate([lax.dynamic_index_in_dim(batches, 1 - group, 0, False), extra], axis=0)
    even = [mine]
    for by in range(2, tiles, 2):
        even.append(swap(other if by & 2 else mine, "tile", by))
    even = jnp.stack(even)
    odd = swap(even, "tile", 1)

    states = layer(True, False, ids, neighbours, even, odd, None, (flat, params))
    for k in range(1, sections):
        a = halves[k - 1]
        states = layer(False, k == sections - 1, ids, neighbours, even, odd, states, (a, swap(a, "tile", 1)))
    kept = states[0]
    back = swap(states[1], "tile", 2)
    out = jnp.where(group == 0, jnp.stack([kept, back]), jnp.stack([back, kept]))
    return out.reshape(activations.shape)


def solution(mesh):
    in_specs = (
        P("section", "tile", None, None, None),
        P("section", None, None, None),
        P("section", None),
        P("section", None),
        P("tile", None, None),
        P(),
    )
    out_specs = P("section", "tile", None, None, None)
    return jax.shard_map(local, mesh=mesh, in_specs=in_specs, out_specs=out_specs, check_vma=False)
```

time: 158 us -> 68.7 us (0.43)
  blocking collectives: 61.5 us -> 0 us
  between operations: 33.8 us -> 0.18 us
  Pallas kernels: 0 us -> 24.1 us
  starting transfers between devices: 2.31 us -> 10.7 us
  matrix products: 8.28 us -> 0 us
  other arithmetic: 7.84 us -> 1 us
  local copies, waits for them, and re-layouts: 7.89 us -> 1.86 us
  waiting for transfers between devices: 35.7 us -> 30.7 us
    all_gather x4 -> x0, blocking collectives: 61.5 us -> none  [advance(): gathered = lax.all_gather(borders[:, None], 'tile', axis=1, tiled=True)]
    pallas_call x0 -> x4, Pallas kernels: none -> 24.1 us  [layer(): pl.pallas_call(functools.partial(layer_kernel, side, tiles, outs, first,...]
    ppermute x4 -> x11, starting transfers between devices: 2.31 us -> 10.7 us  [the longest x8 6.27 us: swap(): return lax.ppermute(value, axis, [(i, i ^ by) for i in range(peers)])]
    dot_general x36 -> x0, matrix products: 8.28 us -> none  [convolve(): jnp.dot(shifted, weight_taps[tap_index], preferred_element_type=jnp.float32)]
    ppermute x4 -> x11, waiting for transfers between devices: 35.7 us -> 30.7 us  [the longest x3 15.9 us: fetch(): lax.ppermute(value, axis, [((i + by) % peers, i) for i in range(peers)])]
    slice x53 -> x1, local copies, waits for them, and re-layouts: 3.59 us -> 0.02 us  [local(): kept = states[0]]
    convert_element_type x15 -> x0, other arithmetic: 3.47 us -> none  [the longest x8 2.03 us: normalize(): (values * lax.rsqrt(mean_sq + 1e-05) * gain_row.astype(jnp.float32)).asty...]
    concatenate x8 -> x2, other arithmetic: 2.39 us -> 0.12 us  [the longest x1 0.11 us: local(): jnp.concatenate([lax.dynamic_index_in_dim(batches, group, 0, False), extr...]
  transfers between devices with their start and end apart: 4 -> 11, of which waited for: 4 -> 4; matrix products, arithmetic and copies ran while one was open for 0% -> 1% of each run, Pallas kernels for 0% -> 30%
where the time goes in v1:
time: 68.7 us; the launch traced here: 68.6 us
  waiting for transfers between devices  30.7 us (45%)
  Pallas kernels  24.1 us (35%)
  starting transfers between devices  10.7 us (16%)
  local copies, waits for them, and re-layouts  1.86 us (3%)
  other arithmetic  1 us (1%)
    pallas_call x4, Pallas kernels, layer(): pl.pallas_call(functools.partial(layer_kernel, side, tiles, outs, first,...  24.1 us
    ppermute x3, waiting for transfers between devices, fetch(): lax.ppermute(value, axis, [((i + by) % peers, i) for i in range(peers)])  15.9 us
    ppermute x8, waiting for transfers between devices, swap(): return lax.ppermute(value, axis, [(i, i ^ by) for i in range(peers)])  14.8 us
    ppermute x8, starting transfers between devices, swap(): return lax.ppermute(value, axis, [(i, i ^ by) for i in range(peers)])  6.27 us
    ppermute x3, starting transfers between devices, fetch(): lax.ppermute(value, axis, [((i + by) % peers, i) for i in range(peers)])  4.47 us
  transfers between devices with their start and end apart: 11, of which 4 were waited for; matrix products, arithmetic and copies ran while one was open for 1% of the time, Pallas kernels for 30%

profile of v1, /device:TPU:0, one launch (start us, length us, event | category | flops | bytes accessed | tf_op | source)
XLA Modules:
  0.0 68.6 jit_solution(2737795867006035779)
XLA Ops:
  0.0 1.1 %constant_dynamic-slice_fusion = bf16[1152,256]{1,0:T(8,128)(2,1)S(1)} fusion(bf16[2304,256]{1,0:T(8,128)(2,1)} %bitcast.17, s32[]{:T(128)S(6)} %select_n.28), kind=kLoop, calls=%fused_computation.10 | loop fusion | bytes 1179652 | tf_op jit(solution)/shard_map/dynamic_slice | solution.py:194
  1.2 0.6 concatenate.33
  1.8 0.0 copy-start
  1.8 0.0 copy-start.1
  1.8 4.0 %collective-permute-start.4 = (bf16[1168,256]{1,0:T(8,128)(2,1)S(1)}, bf16[1168,256]{1,0:T(8,128)(2,1)S(1)}, u32[]{:S(2)}, u32[]{:S(2)}) collective-permute-start(bf16[1168,256]{1,0:T(8,128)(2,1)S(1)} %concatenate.33), channel_id=1, source_target_pairs={{8,0},{16,8},{24,16},{0,24},{9,1},{17,9},{25,17},{1,25},{10,2},{18... | collective-permute-start | bytes 1794056 | tf_op jit(solution)/shard_map/ppermute | solution.py:22
  5.7 0.1 pad.16.clone
  5.9 0.1 fusion
  6.0 1.6 %collective-permute-start = (bf16[272,256]{1,0:T(8,128)(2,1)S(1)}, bf16[272,256]{1,0:T(8,128)(2,1)S(1)}, u32[]{:S(2)}, u32[]{:S(2)}) collective-permute-start(bf16[272,256]{1,0:T(8,128)(2,1)S(1)} %get-tuple-element.10), channel_id=1, source_target_pairs={{0,2},{1,3},{2,0},{3,1},{4,6},{5,7},{6,4},{7,5},{8,10},{9,11},{10,... | collective-permute-start | bytes 417800 | tf_op jit(solution)/shard_map/ppermute | solution.py:17
  7.6 2.6 %collective-permute-start.1 = (bf16[272,256]{1,0:T(8,128)(2,1)S(1)}, bf16[272,256]{1,0:T(8,128)(2,1)S(1)}, u32[]{:S(2)}, u32[]{:S(2)}) collective-permute-start(bf16[272,256]{1,0:T(8,128)(2,1)S(1)} %get-tuple-element.9), channel_id=1, source_target_pairs={{0,4},{1,5},{2,6},{3,7},{4,0},{5,1},{6,2},{7,3},{8,12},{9,13},{10,... | collective-permute-start | bytes 417800 | tf_op jit(solution)/shard_map/ppermute | solution.py:17
  10.2 0.2 collective-permute-start.2
  10.4 0.5 collective-permute-start.6
  10.9 1.9 %collective-permute-done = bf16[272,256]{1,0:T(8,128)(2,1)S(1)} collective-permute-done((bf16[272,256]{1,0:T(8,128)(2,1)S(1)}, bf16[272,256]{1,0:T(8,128)(2,1)S(1)}, u32[]{:S(2)}, u32[]{:S(2)}) %collective-permute-start) | collective-permute-done | bytes 139296 | tf_op jit(solution)/shard_map/ppermute | solution.py:17
  12.8 0.0 collective-permute-start.8
  12.8 8.1 %collective-permute-done.1 = bf16[272,256]{1,0:T(8,128)(2,1)S(1)} collective-permute-done((bf16[272,256]{1,0:T(8,128)(2,1)S(1)}, bf16[272,256]{1,0:T(8,128)(2,1)S(1)}, u32[]{:S(2)}, u32[]{:S(2)}) %collective-permute-start.1) | collective-permute-done | bytes 139296 | tf_op jit(solution)/shard_map/ppermute | solution.py:17
  20.9 0.0 collective-permute-done.2
  20.9 0.1 pad_maximum_fusion.refs_2_
  21.0 0.1 collective-permute-start.3
  21.0 0.0 collective-permute-done.4.refs_5_
  21.1 0.5 collective-permute-start.5
  21.5 15.9 %collective-permute-done.6.refs_5_ = bf16[1168,256]{1,0:T(8,128)(2,1)S(1)} collective-permute-done((bf16[1168,256]{1,0:T(8,128)(2,1)S(1)}, bf16[1168,256]{1,0:T(8,128)(2,1)S(1)}, u32[]{:S(2)}, u32[]{:S(2)}) %collective-permute-start.6) | collective-permute-done | bytes 598048 | tf_op jit(solution)/shard_map/ppermute | solution.py:22
  37.4 0.0 collective-permute-start.7
  37.4 0.1 pad_add_fusion.refs_0_
  37.5 0.6 collective-permute-start.9
  38.1 0.0 collective-permute-done.3.refs_3_
  38.1 6.6 %shard_map.64.refs_4_ = bf16[8,256,256]{2,1,0:T(8,128)(2,1)S(1)} custom-call(s32[2]{0:T(128)S(1)} %pad_add_fusion.refs_0_, s32[3,8,8]{2,1,0:T(8,128)S(1)} %copy-done.1, bf16[4,272,256]{2,1,0:T(8,128)(2,1)S(1)} %pad_maximum_fusion.refs_2_, bf16[4,272,256]{2,1,0:T(8,128)(2,1)S(1)} %collective-permute-done.3.refs_3_, bf16[2304,256]{1,0:T(8,128)(2,1)S(1)} %bitcast.18, ...), custom_call_target="tpu_custom_call" | custom-call | flops 2415919104 | bytes 2097152 | tf_op jit(solution)/shard_map/pallas_call | solution.py:170
  44.8 7.0 %shard_map.65.refs_4_ = bf16[8,256,256]{2,1,0:T(8,128)(2,1)S(1)} custom-call(s32[2]{0:T(128)S(1)} %pad_add_fusion.refs_0_, s32[3,8,8]{2,1,0:T(8,128)S(1)} %copy-done.1, bf16[4,272,256]{2,1,0:T(8,128)(2,1)S(1)} %pad_maximum_fusion.refs_2_, bf16[4,272,256]{2,1,0:T(8,128)(2,1)S(1)} %collective-permute-done.3.refs_3_, ...), custom_call_target="tpu_custom_call" | custom-call | flops 2415919104 | bytes 2097152 | tf_op jit(solution)/shard_map/pallas_call | solution.py:170
  51.8 7.0 %shard_map.66.refs_4_ = bf16[8,256,256]{2,1,0:T(8,128)(2,1)S(1)} custom-call(s32[2]{0:T(128)S(1)} %pad_add_fusion.refs_0_, s32[3,8,8]{2,1,0:T(8,128)S(1)} %copy-done.1, bf16[4,272,256]{2,1,0:T(8,128)(2,1)S(1)} %pad_maximum_fusion.refs_2_, bf16[4,272,256]{2,1,0:T(8,128)(2,1)S(1)} %collective-permute-done.3.refs_3_, ...), custom_call_target="tpu_custom_call" | custom-call | flops 2415919104 | bytes 2097152 | tf_op jit(solution)/shard_map/pallas_call | solution.py:170
  58.8 0.0 collective-permute-done.9.refs_6_
  58.8 3.5 %shard_map.67 = bf16[2,256,256]{2,1,0:T(8,128)(2,1)S(1)} custom-call(s32[2]{0:T(128)S(1)} %pad_add_fusion.refs_0_, s32[3,8,8]{2,1,0:T(8,128)S(1)} %copy-done.1, bf16[4,272,256]{2,1,0:T(8,128)(2,1)S(1)} %pad_maximum_fusion.refs_2_, bf16[4,272,256]{2,1,0:T(8,128)(2,1)S(1)} %collective-permute-done.3.refs_3_, bf16[8,256,256]{2,1,0:T(8,128)(2,1)S(1)} %shard_map.66.refs_4_, ...), custom_call_target="tpu_custom_call" | custom-call | flops 603979776 | bytes 524288 | tf_op jit(solution)/shard_map/pallas_call | solution.py:170
  62.3 0.7 collective-permute-start.10
  63.0 4.8 %collective-permute-done.10 = bf16[256,256]{1,0:T(8,128)(2,1)S(1)} collective-permute-done((bf16[256,256]{1,0:T(8,128)(2,1)S(1)}, bf16[256,256]{1,0:T(8,128)(2,1)S(1)}, u32[]{:S(2)}, u32[]{:S(2)}) %collective-permute-start.10) | collective-permute-done | bytes 131104 | tf_op jit(solution)/shard_map/ppermute | solution.py:17
  67.8 0.7 %maximum_select_fusion = bf16[2,1,16,16,256]{4,3,2,1,0:T(8,128)(2,1)} fusion(bf16[1,1,16,16,256]{4,3,2,1,0:T(8,128)(2,1)S(1)} %bitcast.25, bf16[1,1,16,16,256]{4,3,2,1,0:T(8,128)(2,1)S(1)} %bitcast.20, pred[]{:T(512)S(6)} %eq.3), kind=kLoop, calls=%fused_computation.1 | loop fusion | flops 393216 | bytes 524289 | tf_op jit(solution)/shard_map/jit(_where)/select_n | solution.py:213
  (18 shorter events, 0.1 us)
Async XLA Ops:
  0.0 1.2 %copy-start.4 = (bf16[1,256]{1,0:T(2,128)(2,1)S(1)}, bf16[1,256]{1,0:T(2,128)(2,1)}, u32[]{:S(2)}) copy-start(bf16[1,256]{1,0:T(2,128)(2,1)} %param.8) | copy-start | bytes 1540
  0.0 1.2 %copy-start.5 = (bf16[1,256]{1,0:T(2,128)(2,1)S(1)}, bf16[1,256]{1,0:T(2,128)(2,1)}, u32[]{:S(2)}) copy-start(bf16[1,256]{1,0:T(2,128)(2,1)} %param.9) | copy-start | bytes 1540
  0.0 5.8 %copy-start.2 = (bf16[2,1,16,16,256]{4,3,2,1,0:T(8,128)(2,1)S(1)}, bf16[2,1,16,16,256]{4,3,2,1,0:T(8,128)(2,1)}, u32[]{:S(2)}) copy-start(bf16[2,1,16,16,256]{4,3,2,1,0:T(8,128)(2,1)} %param.6) | copy-start | bytes 786436
  0.0 5.8 %copy-start.3 = (bf16[1,9,256]{2,1,0:T(8,128)(2,1)S(1)}, bf16[1,9,256]{2,1,0:T(8,128)(2,1)}, u32[]{:S(2)}) copy-start(bf16[1,9,256]{2,1,0:T(8,128)(2,1)} %param.10) | copy-start | bytes 13828
  1.8 36.4 %copy-start = (bf16[1,9,256,256]{3,2,1,0:T(8,128)(2,1)S(1)}, bf16[1,9,256,256]{3,2,1,0:T(8,128)(2,1)}, u32[]{:S(2)}) copy-start(bf16[1,9,256,256]{3,2,1,0:T(8,128)(2,1)} %param.7) | copy-start | bytes 3538948
  1.8 36.3 %copy-start.1 = (s32[3,8,8]{2,1,0:T(8,128)S(1)}, s32[3,8,8]{2,1,0:T(8,128)}, u32[]{:S(2)}) copy-start(s32[3,8,8]{2,1,0:T(8,128)} %refs_1_.7) | copy-start | bytes 2308
  1.8 19.3 %collective-permute-start.4 = (bf16[1168,256]{1,0:T(8,128)(2,1)S(1)}, bf16[1168,256]{1,0:T(8,128)(2,1)S(1)}, u32[]{:S(2)}, u32[]{:S(2)}) collective-permute-start(bf16[1168,256]{1,0:T(8,128)(2,1)S(1)} %concatenate.33), channel_id=1, source_target_pairs={{8,0},{16,8},{24,16},{0,24},{9,1},{17,9},{25,17},{1,25},{10,2},{18... | collective-permute-start | bytes 1794056 | tf_op jit(solution)/shard_map/ppermute | solution.py:22
  6.0 6.8 %collective-permute-start = (bf16[272,256]{1,0:T(8,128)(2,1)S(1)}, bf16[272,256]{1,0:T(8,128)(2,1)S(1)}, u32[]{:S(2)}, u32[]{:S(2)}) collective-permute-start(bf16[272,256]{1,0:T(8,128)(2,1)S(1)} %get-tuple-element.10), channel_id=1, source_target_pairs={{0,2},{1,3},{2,0},{3,1},{4,6},{5,7},{6,4},{7,5},{8,10},{9,11},{10,... | collective-permute-start | bytes 417800 | tf_op jit(solution)/shard_map/ppermute | solution.py:17
  7.6 13.3 %collective-permute-start.1 = (bf16[272,256]{1,0:T(8,128)(2,1)S(1)}, bf16[272,256]{1,0:T(8,128)(2,1)S(1)}, u32[]{:S(2)}, u32[]{:S(2)}) collective-permute-start(bf16[272,256]{1,0:T(8,128)(2,1)S(1)} %get-tuple-element.9), channel_id=1, source_target_pairs={{0,4},{1,5},{2,6},{3,7},{4,0},{5,1},{6,2},{7,3},{8,12},{9,13},{10,... | collective-permute-start | bytes 417800 | tf_op jit(solution)/shard_map/ppermute | solution.py:17
  10.2 10.7 %collective-permute-start.2 = (bf16[272,256]{1,0:T(8,128)(2,1)S(1)}, bf16[272,256]{1,0:T(8,128)(2,1)S(1)}, u32[]{:S(2)}, u32[]{:S(2)}) collective-permute-start(bf16[272,256]{1,0:T(8,128)(2,1)S(1)} %get-tuple-element.10), channel_id=1, source_target_pairs={{0,6},{1,7},{2,4},{3,5},{4,2},{5,3},{6,0},{7,1},{8,14},{9,15},{10,... | collective-permute-start | bytes 417800 | tf_op jit(solution)/shard_map/ppermute | solution.py:17
  10.4 27.0 %collective-permute-start.6 = (bf16[1168,256]{1,0:T(8,128)(2,1)S(1)}, bf16[1168,256]{1,0:T(8,128)(2,1)S(1)}, u32[]{:S(2)}, u32[]{:S(2)}) collective-permute-start(bf16[1168,256]{1,0:T(8,128)(2,1)S(1)} %concatenate.33), channel_id=1, source_target_pairs={{16,0},{24,8},{0,16},{8,24},{17,1},{25,9},{1,17},{9,25},{18,2},{26... | collective-permute-start | bytes 1794056 | tf_op jit(solution)/shard_map/ppermute | solution.py:22
  12.8 24.7 %collective-permute-start.8 = (bf16[1168,256]{1,0:T(8,128)(2,1)S(1)}, bf16[1168,256]{1,0:T(8,128)(2,1)S(1)}, u32[]{:S(2)}, u32[]{:S(2)}) collective-permute-start(bf16[1168,256]{1,0:T(8,128)(2,1)S(1)} %concatenate.33), channel_id=1, source_target_pairs={{24,0},{0,8},{8,16},{16,24},{25,1},{1,9},{9,17},{17,25},{26,2},{2,... | collective-permute-start | bytes 1794056 | tf_op jit(solution)/shard_map/ppermute | solution.py:22
  21.0 17.2 %collective-permute-start.3 = (bf16[4,272,256]{2,1,0:T(8,128)(2,1)S(1)}, bf16[4,272,256]{2,1,0:T(8,128)(2,1)S(1)}, u32[]{:S(2)}, u32[]{:S(2)}) collective-permute-start(bf16[4,272,256]{2,1,0:T(8,128)(2,1)S(1)} %pad_maximum_fusion.refs_2_), channel_id=1, source_target_pairs={{0,1},{1,0},{2,3},{3,2},{4,5},{5,4},{6,7},{7,6},{8,9},{9,8},{10,11... | collective-permute-start | bytes 1671176 | tf_op jit(solution)/shard_map/ppermute | solution.py:17
  21.1 23.7 %collective-permute-start.5 = (bf16[1168,256]{1,0:T(8,128)(2,1)S(1)}, bf16[1168,256]{1,0:T(8,128)(2,1)S(1)}, u32[]{:S(2)}, u32[]{:S(2)}) collective-permute-start(bf16[1168,256]{1,0:T(8,128)(2,1)S(1)} %collective-permute-done.4.refs_5_), channel_id=1, source_target_pairs={{0,1},{1,0},{2,3},{3,2},{4,5},{5,4},{6,7},{7,6},{8,9},{9,8},{10,11... | collective-permute-start | bytes 1794056 | tf_op jit(solution)/shard_map/ppermute | solution.py:17
  37.4 14.3 %collective-permute-start.7 = (bf16[1168,256]{1,0:T(8,128)(2,1)S(1)}, bf16[1168,256]{1,0:T(8,128)(2,1)S(1)}, u32[]{:S(2)}, u32[]{:S(2)}) collective-permute-start(bf16[1168,256]{1,0:T(8,128)(2,1)S(1)} %collective-permute-done.6.refs_5_), channel_id=1, source_target_pairs={{0,1},{1,0},{2,3},{3,2},{4,5},{5,4},{6,7},{7,6},{8,9},{9,8},{10,11... | collective-permute-start | bytes 1794056 | tf_op jit(solution)/shard_map/ppermute | solution.py:17
  37.5 21.3 %collective-permute-start.9 = (bf16[1168,256]{1,0:T(8,128)(2,1)S(1)}, bf16[1168,256]{1,0:T(8,128)(2,1)S(1)}, u32[]{:S(2)}, u32[]{:S(2)}) collective-permute-start(bf16[1168,256]{1,0:T(8,128)(2,1)S(1)} %collective-permute-done.8.refs_5_), channel_id=1, source_target_pairs={{0,1},{1,0},{2,3},{3,2},{4,5},{5,4},{6,7},{7,6},{8,9},{9,8},{10,11... | collective-permute-start | bytes 1794056 | tf_op jit(solution)/shard_map/ppermute | solution.py:17
  62.3 5.5 %collective-permute-start.10 = (bf16[256,256]{1,0:T(8,128)(2,1)S(1)}, bf16[256,256]{1,0:T(8,128)(2,1)S(1)}, u32[]{:S(2)}, u32[]{:S(2)}) collective-permute-start(bf16[256,256]{1,0:T(8,128)(2,1)S(1)} %get-tuple-element.6), channel_id=1, source_target_pairs={{0,2},{1,3},{2,0},{3,1},{4,6},{5,7},{6,4},{7,5},{8,10},{9,11},{10,... | collective-permute-start | bytes 393224 | tf_op jit(solution)/shard_map/ppermute | solution.py:17

commit v2 on v0

v2 whole, which is shorter than its diff:
```python
import functools
import math

import jax
import jax.numpy as jnp
from jax import lax
from jax.experimental import pallas as pl
from jax.experimental.pallas import tpu as pltpu
from jax.sharding import PartitionSpec as P

BF16 = jnp.bfloat16
F32 = jnp.float32
EXTRA = 16
LANES = 128


def swap(value, axis, by):
    peers = lax.axis_size(axis)
    return lax.ppermute(value, axis, [(i, i ^ by) for i in range(peers)])


def fetch(value, axis, by):
    peers = lax.axis_size(axis)
    return lax.ppermute(value, axis, [((i + by) % peers, i) for i in range(peers)])


def ring_lines(side, depth):
    lines = []
    for d in range(depth):
        lines += [("row", d), ("row", side - 1 - d), ("col", d), ("col", side - 1 - d)]
    return lines


def weight_copies(core, half_a, half_b, w, par, sem):
    rows = half_a.shape[0] - EXTRA
    at_a = pl.multiple_of(core * rows, LANES)
    at_b = pl.multiple_of((1 - core) * rows, LANES)
    return [
        pltpu.make_async_copy(half_a.at[pl.ds(0, rows)], w.at[pl.ds(at_a, rows)], sem.at[0]),
        pltpu.make_async_copy(half_b.at[pl.ds(0, rows)], w.at[pl.ds(at_b, rows)], sem.at[1]),
        pltpu.make_async_copy(half_a.at[pl.ds(rows, EXTRA)], par, sem.at[2]),
    ]


def layer_kernel(side, tiles, source, depth_in, depth_out, started, *refs):
    refs = list(refs)
    take = lambda n: [refs.pop(0) for _ in range(n)]
    px = side * side
    ids, near = take(2)
    if source == "payload":
        even, odd = take(2)
    elif source == "full":
        even, odd, mt = take(3)
    else:
        kept_in, lines_in, mt = take(3)
    copied = source != "payload"
    weights = take(2)
    outs = take(2 if depth_out is None and source == "payload" or depth_out else 1)
    if copied:
        w, par, sem = take(3)
    else:
        w, par = weights
    zf, vtmp, vlines, fr, cr, pads, x, acc, xo, acco = take(10)
    if source == "payload":
        mt = outs[1]
    ch = x.shape[1] // 9
    halves = ch // LANES
    own, core = ids[0], ids[1]
    lines_out = ring_lines(side, depth_out or 0)
    step = min(64, px)
    chunks = [slice(i, i + step) for i in range(0, px, step)]

    if copied:
        copies = weight_copies(core, *weights, w, par, sem)
        if not started:
            for copy in copies:
                copy.start()
        copies[2].wait()
    gain = par[0:1, :].astype(F32)
    bias = par[1:2, :].astype(F32)

    def normed(part):
        mean_sq = jnp.mean(part * part, axis=-1, keepdims=True)
        return (part * lax.rsqrt(mean_sq + 1e-05) * gain).astype(BF16).astype(F32)

    def by_lanes(value):
        return [value[:, h * LANES : (h + 1) * LANES] for h in range(halves)]

    def at_line(kind, at):
        return pl.ds(at * side, side) if kind == "row" else pl.ds(at, side, stride=side)

    def normed_tile(b, read):
        for part in chunks:
            v = read(part)
            for h, value in enumerate(by_lanes(normed(v))):
                zf[b, h, part] = value
            if depth_out:
                for h, value in enumerate(by_lanes(v)):
                    vtmp[h, part] = value
        for n, (kind, at) in enumerate(lines_out):
            for h in range(halves):
                vlines[b, n, :, h * LANES : (h + 1) * LANES] = vtmp[h, at_line(kind, at), :].astype(BF16)

    def other(i):
        return jnp.where(i == 0, 1, i + 2)

    if source == "payload":

        @pl.loop(0, tiles // 2)
        def _(j):
            for ref, b in ((even, 2 * j), (odd, 2 * j + 1)):
                normed_tile(b, lambda part: ref[j, part].astype(F32))
                mt[b, :, 0:EXTRA] = jnp.transpose(ref[j, px : px + EXTRA, :].astype(F32))

    elif source == "full":

        @pl.loop(0, tiles // 2)
        def _(j):
            for ref, b in ((even, 2 * j), (odd, 2 * j + 1)):
                normed_tile(b, lambda part: ref[j, part].astype(F32))

    else:
        for place in range(2):
            for part in chunks:
                for h, value in enumerate(by_lanes(normed(kept_in[place, part].astype(F32)))):
                    zf[2 * place, h, part] = value
        lines = ring_lines(side, depth_in)

        @pl.loop(0, tiles - 2)
        def _(i):
            b = other(i)
            for first in range(0, len(lines), 4):
                z = normed(lines_in[i, first : first + 4].astype(F32).reshape(4 * side, ch))
                for n in range(4):
                    kind, at = lines[first + n]
                    for h, value in enumerate(by_lanes(z[n * side : (n + 1) * side])):
                        zf[b, h, at_line(kind, at), :] = value

    if copied:
        copies[0].wait()
        copies[1].wait()

    place_of = lax.broadcasted_iota(jnp.int32, (side, LANES), 0)
    eight = lax.broadcasted_iota(jnp.int32, (8, LANES), 0)
    first_place, last_place = place_of == 0, place_of == side - 1

    def frames(b):
        tile = own ^ b
        for s in range(4):
            src = own ^ near[0, tile, s]
            which = near[1, tile, s]
            flip = near[2, tile, s] == 1
            by_row = (which == 0) | (which == 2)
            at_row = pl.multiple_of(jnp.where(which == 0, 0, px - side), side)
            at_col = jnp.where(which == 1, side - 1, 0)
            for h in range(halves):
                line = jnp.where(by_row, zf[src, h, pl.ds(at_row, side), :], zf[src, h, pl.ds(at_col, side, stride=side), :])
                groups = [line[g : g + 8] for g in range(0, side, 8)]
                for n, group in enumerate(groups):
                    turned = pltpu.roll(groups[-1 - n], 4, 0)
                    for bit in (2, 1):
                        turned = jnp.where(eight & bit != 0, pltpu.roll(turned, bit, 0), pltpu.roll(turned, 8 - bit, 0))
                    fr[s, h, 8 * n : 8 * n + 8] = jnp.where(flip, turned, group)
        for k in range(4):
            src = own ^ near[0, tile, 4 + k]
            which = near[1, tile, 4 + k]
            at = jnp.where(which < 2, 0, px - side) + jnp.where((which == 1) | (which == 2), side - 1, 0)
            for h in range(halves):
                cr[k, h] = zf[src, h, pl.ds(at, 1), :]

    def spread(place, n, h, line, before, after):
        lanes = slice(h * LANES, (h + 1) * LANES)
        pads[place, n, 0, :, lanes] = jnp.where(first_place, before, pltpu.roll(line, 1, 0)).astype(BF16)
        pads[place, n, 1, :, lanes] = line.astype(BF16)
        pads[place, n, 2, :, lanes] = jnp.where(last_place, after, pltpu.roll(line, side - 1, 0)).astype(BF16)

    def spread_line(place, n, b, kind, at):
        low, high = (3, 1) if kind == "row" else (0, 2)
        for h in range(halves):
            if at < 0 or at >= side:
                edge = {("row", -1): (0, 0, 1), ("row", side): (2, 3, 2), ("col", -1): (3, 0, 3), ("col", side): (1, 1, 2)}
                s, k_before, k_after = edge[kind, at]
                spread(place, n, h, fr[s, h], cr[k_before, h], cr[k_after, h])
            else:
                line = zf[b, h, at_line(kind, at), :]
                spread(place, n, h, line, fr[low, h, at : at + 1], fr[high, h, at : at + 1])

    def build_tile(b, place):
        frames(b)
        for at in range(-1, side + 1):
            spread_line(place, at + 1, b, "row", at)
        metric = mt[b]
        for q in range(9):
            a, c = q // 3, q % 3
            taps = jnp.broadcast_to(metric[:, q : q + 1], (px, LANES)).astype(BF16)
            for lane in range(0, ch, LANES):
                x[place * px : (place + 1) * px, q * ch + lane : q * ch + lane + LANES] = (
                    pads[place, a : a + side, c, :, lane : lane + LANES].reshape(px, LANES) * taps
                )

    def build_lines(b, i):
        frames(b)
        slots = {}
        for kind, at in lines_out:
            for near_at in (at - 1, at, at + 1):
                if (kind, near_at) not in slots:
                    slots[kind, near_at] = len(slots)
                    spread_line(0, slots[kind, near_at], b, kind, near_at)
        for n, (kind, at) in enumerate(lines_out):
            metric = mt[b, at_line(kind, at), :]
            row = pl.multiple_of((i * len(lines_out) + n) * side, side)
            for q in range(9):
                a, c = q // 3, q % 3
                slot, seen = (slots[kind, at + a - 1], c) if kind == "row" else (slots[kind, at + c - 1], a)
                taps = jnp.broadcast_to(metric[:, q : q + 1], (side, LANES)).astype(BF16)
                for lane in range(0, ch, LANES):
                    lanes = slice(lane, lane + LANES)
                    xo[pl.ds(row, side), q * ch + lane : q * ch + lane + LANES] = pads[0, slot, seen, :, lanes] * taps

    def updated(v, conv):
        u = conv + bias
        return (v.astype(F32) + u / (1.0 + jnp.exp(-u))).astype(BF16)

    if depth_out is None:

        @pl.loop(0, tiles // 4)
        def _(j):
            build_tile(4 * j, 0)
            build_tile(4 * j + 2, 1)
            acc[...] = jnp.dot(x[...], w[...], preferred_element_type=F32)
            for place in range(2):
                for part in chunks:
                    conv = acc[place * px + part.start : place * px + part.stop]
                    outs[0][2 * j + place, part] = updated(even[2 * j + place, part], conv)

    else:
        build_tile(0, 0)
        build_tile(2, 1)
        acc[...] = jnp.dot(x[...], w[...], preferred_element_type=F32)
        for place in range(2):
            for part in chunks:
                v = even[place, part] if source == "full" else kept_in[place, part]
                outs[0][place, part] = updated(v, acc[place * px + part.start : place * px + part.stop])
        if depth_out:

            @pl.loop(0, tiles - 2)
            def _(i):
                build_lines(other(i), i)

            acco[...] = jnp.dot(xo[...], w[...], preferred_element_type=F32)

            @pl.loop(0, tiles - 2)
            def _(i):
                count = len(lines_out)
                for first in range(0, count, 4):
                    v = vlines[other(i), first : first + 4] if source == "full" else lines_in[i, first : first + 4]
                    at = pl.multiple_of((i * count + first) * side, side)
                    new = updated(v.reshape(4 * side, ch), acco[pl.ds(at, 4 * side)])
                    outs[1][i, first : first + 4] = new.reshape(4, side, ch)


def pack_kernel(ids, batches, metric, flat, gain, bias, mine, other, half, sem):
    px, ch = batches.shape[1:]
    rows = half.shape[0] - EXTRA
    start = pl.multiple_of(ids[1] * rows, LANES)
    copies = [
        pltpu.make_async_copy(batches.at[ids[2]], mine.at[pl.ds(0, px)], sem.at[0]),
        pltpu.make_async_copy(batches.at[1 - ids[2]], other.at[pl.ds(0, px)], sem.at[1]),
        pltpu.make_async_copy(flat.at[pl.ds(start, rows)], half.at[pl.ds(0, rows)], sem.at[2]),
    ]
    for copy in copies:
        copy.start()
    spare = jnp.concatenate([metric[...], jnp.zeros((EXTRA - 9, px), BF16)], axis=0)
    mine[px : px + EXTRA, :] = spare
    other[px : px + EXTRA, :] = spare
    half[rows : rows + EXTRA, :] = jnp.concatenate([gain[...], bias[...], jnp.zeros((EXTRA - 2, ch), BF16)], axis=0)
    for copy in copies:
        copy.wait()


def pack(ids, batches, metric, flat, gain, bias):
    state = jax.ShapeDtypeStruct((batches.shape[1] + EXTRA, batches.shape[2]), BF16)
    half = jax.ShapeDtypeStruct((flat.shape[0] // 2 + EXTRA, flat.shape[1]), BF16)
    return pl.pallas_call(
        pack_kernel,
        out_shape=(state, state, half),
        in_specs=[SMEM, HBM, VMEM, HBM, VMEM, VMEM],
        out_specs=(VMEM, VMEM, VMEM),
        scratch_shapes=[pltpu.SemaphoreType.DMA((3,))],
        compiler_params=pltpu.CompilerParams(vmem_limit_bytes=60 * 2**20),
    )(ids, batches, metric, flat, gain, bias)


VMEM = pl.BlockSpec(memory_space=pltpu.VMEM)
SMEM = pl.BlockSpec(memory_space=pltpu.SMEM)
HBM = pl.BlockSpec(memory_space=pl.ANY)


def last_layers_kernel(side, tiles, *refs):
    ids, near, even, odd, mt, a3, b3, a4, b4, out, kept, lines = refs[:12]
    w3, par3, sem3, w4, par4, sem4 = refs[12:18]
    space = refs[18:]
    for copy in weight_copies(ids[1], a3, b3, w3, par3, sem3) + weight_copies(ids[1], a4, b4, w4, par4, sem4):
        copy.start()
    layer_kernel(side, tiles, "full", None, 1, True, ids, near, even, odd, mt, a3, b3, kept, lines, w3, par3, sem3, *space)
    layer_kernel(side, tiles, "ring", 1, 0, True, ids, near, kept, lines, mt, a4, b4, out, w4, par4, sem4, *space)


def work_space(side, tiles, ch, depth_out):
    px = side * side
    halves = ch // LANES
    lines = 4 * depth_out if depth_out else 1
    line_rows = lines * side * (tiles - 2) if depth_out else 2 * side
    return [
        pltpu.VMEM((tiles, halves, px, LANES), F32),
        pltpu.VMEM((halves, px, LANES), F32),
        pltpu.VMEM((tiles, lines, side, ch), BF16),
        pltpu.VMEM((4, halves, side, LANES), F32),
        pltpu.VMEM((4, halves, 1, LANES), F32),
        pltpu.VMEM((2, side + 2, 3, side, ch), BF16),
        pltpu.VMEM((2 * px, 9 * ch), BF16),
        pltpu.VMEM((2 * px, ch), F32),
        pltpu.VMEM((line_rows, 9 * ch), BF16),
        pltpu.VMEM((line_rows, ch), F32),
    ]


def weight_space(ch):
    return [pltpu.VMEM((9 * ch, ch), BF16), pltpu.VMEM((EXTRA, ch), BF16), pltpu.SemaphoreType.DMA((3,))]


def limit(operands, scratch):
    sizes = [math.prod(item.shape) * jnp.dtype(item.dtype).itemsize for item in operands]
    sizes += [math.prod(item.shape) * jnp.dtype(item.dtype).itemsize for item in scratch if item.memory_space == pltpu.VMEM]
    return sum(sizes) + 6 * 2**20


def last_layers(side, tiles, ids, near, even, odd, mt, weights):
    ch = even.shape[-1]
    px = side * side
    kept = (2, px, ch)
    scratch = [pltpu.VMEM(kept, BF16), pltpu.VMEM((tiles - 2, 4, side, ch), BF16)]
    scratch += weight_space(ch) + weight_space(ch) + work_space(side, tiles, ch, 1)
    return pl.pallas_call(
        functools.partial(last_layers_kernel, side, tiles),
        out_shape=jax.ShapeDtypeStruct(kept, BF16),
        in_specs=[SMEM, SMEM, VMEM, VMEM, VMEM] + [HBM] * 4,
        out_specs=VMEM,
        scratch_shapes=scratch,
        compiler_params=pltpu.CompilerParams(vmem_limit_bytes=limit((even, odd, mt), scratch)),
        cost_estimate=pl.CostEstimate(flops=1, bytes_accessed=1, transcendentals=0),
    )(ids, near, even, odd, mt, *weights)


def layer(side, tiles, source, depth_in, depth_out, ids, near, data, weights):
    ch = weights[0].shape[-1]
    px = side * side
    halves = ch // LANES
    copied = source != "payload"
    if depth_out is None:
        shapes = [jax.ShapeDtypeStruct((tiles // 2, px, ch), BF16)]
        if not copied:
            shapes.append(jax.ShapeDtypeStruct((tiles, px, LANES), F32))
    else:
        shapes = [jax.ShapeDtypeStruct((2, px, ch), BF16)]
        if depth_out:
            shapes.append(jax.ShapeDtypeStruct((tiles - 2, 4 * depth_out, side, ch), BF16))
    scratch = (weight_space(ch) if copied else []) + work_space(side, tiles, ch, depth_out)
    return pl.pallas_call(
        functools.partial(layer_kernel, side, tiles, source, depth_in, depth_out, False),
        out_shape=shapes,
        in_specs=[SMEM, SMEM] + [VMEM] * len(data) + [HBM if copied else VMEM] * 2,
        out_specs=[VMEM] * len(shapes),
        scratch_shapes=scratch,
        compiler_params=pltpu.CompilerParams(vmem_limit_bytes=limit((*data, *weights, *shapes), scratch)),
        cost_estimate=pl.CostEstimate(flops=1, bytes_accessed=1, transcendentals=0),
    )(ids, near, *data, *weights)


def local(activations, weight, conv_bias, norm_gain, metric, neighbours):
    sections = lax.axis_size("section")
    tiles = lax.axis_size("tile")
    own = lax.axis_index("tile")
    core = own & 1
    group = (own >> 1) & 1
    side, ch = activations.shape[2], activations.shape[-1]
    px = side * side
    ids = jnp.stack([own, core, group]).astype(jnp.int32)

    flat = weight.reshape(-1, ch)
    mine, other, half = pack(ids, activations.reshape(2, px, ch), metric.reshape(9, px), flat, norm_gain, conv_bias)
    arrived = [fetch(half, "section", k) for k in range(1, sections)]

    going = neighbours[0, 0, 0] >= 0

    def fenced(step, *operands):
        shape = jax.eval_shape(step, *operands)
        blank = lambda *_: jax.tree.map(lambda leaf: jnp.zeros(leaf.shape, leaf.dtype), shape)
        return lax.cond(going, step, blank, *operands)

    even = [mine]
    for by in range(2, tiles, 2):
        even.append(swap(other if by & 2 else mine, "tile", by))
    even = jnp.stack(even)
    odd = swap(even, "tile", 1)

    def begin(even, odd):
        return layer(side, tiles, "payload", None, None, ids, neighbours, (even, odd), (flat, half[-EXTRA:]))

    states, spread_metric = fenced(begin, even, odd)
    for k in range(1, sections - 2):

        def proceed(states, spread_metric, a):
            weights = (a, swap(a, "tile", 1))
            data = (states, swap(states, "tile", 1), spread_metric)
            return layer(side, tiles, "full", None, None, ids, neighbours, data, weights)[0]

        states = fenced(proceed, states, spread_metric, arrived[k - 1])

    def finish(states, spread_metric, a, b):
        weights = (a, swap(a, "tile", 1), b, swap(b, "tile", 1))
        return last_layers(side, tiles, ids, neighbours, states, swap(states, "tile", 1), spread_metric, weights)

    done = fenced(finish, states, spread_metric, arrived[-2], arrived[-1])
    back = swap(done[1], "tile", 2)
    out = jnp.where(group == 0, jnp.stack([done[0], back]), jnp.stack([back, done[0]]))
    return out.reshape(activations.shape)


def solution(mesh):
    in_specs = (
        P("section", "tile", None, None, None),
        P("section", None, None, None),
        P("section", None),
        P("section", None),
        P("tile", None, None),
        P(),
    )
    out_specs = P("section", "tile", None, None, None)
    return jax.shard_map(local, mesh=mesh, in_specs=in_specs, out_specs=out_specs, check_vma=False)
```

time: 158 us -> 58.1 us (0.37)
  blocking collectives: 61.5 us -> 0 us
  between operations: 33.8 us -> 0.73 us
  Pallas kernels: 0 us -> 20.9 us
  waiting for transfers between devices: 35.7 us -> 20 us
  starting transfers between devices: 2.31 us -> 13.2 us
  matrix products: 8.28 us -> 0 us
  local copies, waits for them, and re-layouts: 7.89 us -> 1.24 us
  other arithmetic: 7.84 us -> 1.78 us
    all_gather x4 -> x0, blocking collectives: 61.5 us -> none  [advance(): gathered = lax.all_gather(borders[:, None], 'tile', axis=1, tiled=True)]
    pallas_call x0 -> x4, Pallas kernels: none -> 20.9 us  [the longest x2 9.08 us: layer(): pl.pallas_call(functools.partial(layer_kernel, side, tiles, source, depth...]
    ppermute x4 -> x13, waiting for transfers between devices: 35.7 us -> 20 us  [the longest x10 17 us: swap(): return lax.ppermute(value, axis, [(i, i ^ by) for i in range(peers)])]
    ppermute x4 -> x13, starting transfers between devices: 2.31 us -> 13.2 us  [the longest x10 8.37 us: swap(): return lax.ppermute(value, axis, [(i, i ^ by) for i in range(peers)])]
    dot_general x36 -> x0, matrix products: 8.28 us -> none  [convolve(): jnp.dot(shifted, weight_taps[tap_index], preferred_element_type=jnp.float32)]
    convert_element_type x15 -> x0, other arithmetic: 3.47 us -> none  [the longest x8 2.03 us: normalize(): (values * lax.rsqrt(mean_sq + 1e-05) * gain_row.astype(jnp.float32)).asty...]
    concatenate x8 -> x0, other arithmetic: 2.39 us -> none  [the longest x4 1.42 us: assemble(): return jnp.concatenate([top_row[:, None], middle, bottom[:, None]], axis=1)]
    slice x53 -> x3, local copies, waits for them, and re-layouts: 3.59 us -> 1.23 us  [the longest x1 0.7 us: begin(): half[-EXTRA:]]
  transfers between devices with their start and end apart: 4 -> 13, of which waited for: 4 -> 9; matrix products, arithmetic and copies ran while one was open for 0% -> 4% of each run, Pallas kernels for 0% -> 16%
where the time goes in v2:
time: 58.1 us; the launch traced here: 57.9 us
  Pallas kernels  20.9 us (36%)
  waiting for transfers between devices  20 us (34%)
  starting transfers between devices  13.2 us (23%)
  other arithmetic  1.78 us (3%)
  local copies, waits for them, and re-layouts  1.24 us (2%)
  between operations  0.73 us (1%)
    ppermute x10, waiting for transfers between devices, swap(): return lax.ppermute(value, axis, [(i, i ^ by) for i in range(peers)])  17 us
    pallas_call x2, Pallas kernels, layer(): pl.pallas_call(functools.partial(layer_kernel, side, tiles, source, depth...  9.08 us
    pallas_call x1, Pallas kernels, last_layers(): pl.pallas_call(functools.partial(last_layers_kernel, side, tiles), out_sh...  8.85 us
    ppermute x10, starting transfers between devices, swap(): return lax.ppermute(value, axis, [(i, i ^ by) for i in range(peers)])  8.37 us
    ppermute x3, starting transfers between devices, fetch(): lax.ppermute(value, axis, [((i + by) % peers, i) for i in range(peers)])  4.79 us
    ppermute x3, waiting for transfers between devices, fetch(): lax.ppermute(value, axis, [((i + by) % peers, i) for i in range(peers)])  2.98 us
    pallas_call x1, Pallas kernels, pack(): pl.pallas_call(pack_kernel, out_shape=(state, state, half), in_specs=[SME...  2.97 us
  transfers between devices with their start and end apart: 13, of which 9 were waited for; matrix products, arithmetic and copies ran while one was open for 4% of the time, Pallas kernels for 16%

profile of v2, /device:TPU:0, one launch (start us, length us, event | category | flops | bytes accessed | tf_op | source)
XLA Modules:
  0.0 57.9 jit_solution(13664227183177929527)
XLA Ops:
  0.0 0.1 pad_add_fusion.ids
  0.1 3.0 %shard_map.64 = (bf16[272,256]{1,0:T(8,128)(2,1)}, bf16[272,256]{1,0:T(8,128)(2,1)}, bf16[1168,256]{1,0:T(8,128)(2,1)}) custom-call(s32[3]{0:T(128)S(1)} %pad_add_fusion.ids, bf16[2,256,256]{2,1,0:T(8,128)(2,1)} %bitcast.18, bf16[9,256]{1,0:T(8,128)(2,1)} %bitcast.24, bf16[2304,256]{1,0:T(8,128)(2,1)} %bitcast.15, bf16[1,256]{1,0:T(2,128)(2,1)} %gain.1, ...), custom_call_target="tpu_custom_call" | custom-call | tf_op jit(solution)/shard_map/pallas_call | solution.py:284
  3.1 5.1 %collective-permute-start.7 = (bf16[272,256]{1,0:T(8,128)(2,1)}, bf16[272,256]{1,0:T(8,128)(2,1)S(1)}, u32[]{:S(2)}, u32[]{:S(2)}) collective-permute-start(bf16[272,256]{1,0:T(8,128)(2,1)} %get-tuple-element.69), channel_id=1, source_target_pairs={{0,6},{1,7},{2,4},{3,5},{4,2},{5,3},{6,0},{7,1},{8,14},{9,15},{10,... | collective-permute-start | bytes 417800 | tf_op jit(solution)/shard_map/ppermute | solution.py:19
  8.2 0.6 %collective-permute-start.6 = (bf16[272,256]{1,0:T(8,128)(2,1)}, bf16[272,256]{1,0:T(8,128)(2,1)S(1)}, u32[]{:S(2)}, u32[]{:S(2)}) collective-permute-start(bf16[272,256]{1,0:T(8,128)(2,1)} %get-tuple-element.68), channel_id=1, source_target_pairs={{0,4},{1,5},{2,6},{3,7},{4,0},{5,1},{6,2},{7,3},{8,12},{9,13},{10,... | collective-permute-start | bytes 417800 | tf_op jit(solution)/shard_map/ppermute | solution.py:19
  8.8 2.6 %collective-permute-start.9 = (bf16[1168,256]{1,0:T(8,128)(2,1)}, bf16[1168,256]{1,0:T(8,128)(2,1)}, u32[]{:S(2)}, u32[]{:S(2)}) collective-permute-start(bf16[1168,256]{1,0:T(8,128)(2,1)} %get-tuple-element.67), channel_id=1, source_target_pairs={{8,0},{16,8},{24,16},{0,24},{9,1},{17,9},{25,17},{1,25},{10,2},{18... | collective-permute-start | bytes 1794056 | tf_op jit(solution)/shard_map/ppermute | solution.py:24
  11.4 0.5 collective-permute-start.10
  11.9 1.0 %collective-permute-done.7 = bf16[272,256]{1,0:T(8,128)(2,1)S(1)} collective-permute-done((bf16[272,256]{1,0:T(8,128)(2,1)}, bf16[272,256]{1,0:T(8,128)(2,1)S(1)}, u32[]{:S(2)}, u32[]{:S(2)}) %collective-permute-start.7) | collective-permute-done | bytes 139296 | tf_op jit(solution)/shard_map/ppermute | solution.py:19
  12.9 1.7 %collective-permute-start.11 = (bf16[1168,256]{1,0:T(8,128)(2,1)}, bf16[1168,256]{1,0:T(8,128)(2,1)}, u32[]{:S(2)}, u32[]{:S(2)}) collective-permute-start(bf16[1168,256]{1,0:T(8,128)(2,1)} %get-tuple-element.67), channel_id=1, source_target_pairs={{24,0},{0,8},{8,16},{16,24},{25,1},{1,9},{9,17},{17,25},{26,2},{2,... | collective-permute-start | bytes 1794056 | tf_op jit(solution)/shard_map/ppermute | solution.py:24
  14.6 1.5 %collective-permute-done.5 = bf16[272,256]{1,0:T(8,128)(2,1)S(1)} collective-permute-done((bf16[272,256]{1,0:T(8,128)(2,1)}, bf16[272,256]{1,0:T(8,128)(2,1)S(1)}, u32[]{:S(2)}, u32[]{:S(2)}) %collective-permute-start.5) | collective-permute-done | bytes 139296 | tf_op jit(solution)/shard_map/ppermute | solution.py:19
  16.1 4.0 %collective-permute-done.6 = bf16[272,256]{1,0:T(8,128)(2,1)S(1)} collective-permute-done((bf16[272,256]{1,0:T(8,128)(2,1)}, bf16[272,256]{1,0:T(8,128)(2,1)S(1)}, u32[]{:S(2)}, u32[]{:S(2)}) %collective-permute-start.6) | collective-permute-done | bytes 139296 | tf_op jit(solution)/shard_map/ppermute | solution.py:19
  20.2 1.0 %pad_maximum_fusion = bf16[4,272,256]{2,1,0:T(8,128)(2,1)S(1)} fusion(bf16[1,272,256]{2,1,0:T(8,128)(2,1)S(1)} %bitcast.20, bf16[1,272,256]{2,1,0:T(8,128)(2,1)S(1)} %bitcast.22, bf16[1,272,256]{2,1,0:T(8,128)(2,1)S(1)} %bitcast.21, bf16[1,272,256]{2,1,0:T(8,128)(2,1)} %bitcast.19), kind=kLoop, calls=%fused_computation | loop fusion | flops 835584 | bytes 1114112 | tf_op jit(solution)/shard_map/stack | solution.py:404
  21.1 0.1 collective-permute-start.8
  21.2 0.5 slice.13
  22.4 0.8 %collective-permute-done.8 = bf16[4,272,256]{2,1,0:T(8,128)(2,1)S(1)} collective-permute-done((bf16[4,272,256]{2,1,0:T(8,128)(2,1)S(1)}, bf16[4,272,256]{2,1,0:T(8,128)(2,1)S(1)}, u32[]{:S(2)}, u32[]{:S(2)}) %collective-permute-start.8) | collective-permute-done | bytes 557088 | tf_op jit(solution)/shard_map/ppermute | solution.py:19
  23.2 4.8 %conditional.3 = ((bf16[4,256,256]{2,1,0:T(8,128)(2,1)S(1)}, f32[8,256,128]{2,1,0:T(8,128)S(1)})) conditional(s32[]{:T(128)} %bitcast, () %tuple.26, (bf16[1168,256]{1,0:T(8,128)(2,1)}, s32[3]{0:T(128)S(1)}, s32[3,8,8]{2,1,0:T(8,128)S(1)}, bf16[4,272,256]{2,1,0:T(8,128)(2,1)S(1)}, bf16[4,272,256]{2,1,0:T(8,128)(2,1)S(1)}, ...), branch_computations={%region_0.0_spmd, %region_1.0_spmd} | conditional | flops 1 | bytes 1572894 | solution.py:399
  23.2 0.7 %slice.4.refs_5_ = bf16[16,256]{1,0:T(8,128)(2,1)S(1)} slice(bf16[1168,256]{1,0:T(8,128)(2,1)} %get-tuple-element.50), slice={[1152:1168], [0:256]} | slice | bytes 16384 | tf_op jit(solution)/shard_map/cond/branch_1_fun/slice | solution.py:408
  23.9 4.2 %branch_1_fun.3 = (bf16[4,256,256]{2,1,0:T(8,128)(2,1)S(1)}, f32[8,256,128]{2,1,0:T(8,128)S(1)}) custom-call(s32[3]{0:T(128)S(1)} %get-tuple-element.44.refs_0_, s32[3,8,8]{2,1,0:T(8,128)S(1)} %get-tuple-element.46.refs_1_, bf16[4,272,256]{2,1,0:T(8,128)(2,1)S(1)} %get-tuple-element.47.refs_2_, bf16[4,272,256]{2,1,0:T(8,128)(2,1)S(1)} %get-tuple-element.48.refs_3_, ...), custom_call_target="tpu_custom_call" | custom-call | flops 1 | bytes 1 | tf_op jit(solution)/shard_map/cond/branch_1_fun/pallas_call | solution.py:369
  28.0 7.8 %conditional.4 = (bf16[4,256,256]{2,1,0:T(8,128)(2,1)S(1)}) conditional(s32[]{:T(128)} %bitcast, () %tuple.25, (bf16[4,256,256]{2,1,0:T(8,128)(2,1)S(1)}, bf16[1168,256]{1,0:T(8,128)(2,1)}, s32[3]{0:T(128)S(1)}, s32[3,8,8]{2,1,0:T(8,128)S(1)}, f32[8,256,128]{2,1,0:T(8,128)S(1)}) %tuple.41), branch_computations={%region_2.0_spmd, %region_3.0_spmd} | conditional | flops 1 | bytes 4489305 | solution.py:399
  28.1 0.2 collective-permute-start.1
  28.3 0.4 collective-permute-start
  28.6 2.3 %collective-permute-done.refs_3_ = bf16[4,256,256]{2,1,0:T(8,128)(2,1)S(1)} collective-permute-done((bf16[4,256,256]{2,1,0:T(8,128)(2,1)S(1)}, bf16[4,256,256]{2,1,0:T(8,128)(2,1)S(1)}, u32[]{:S(2)}, u32[]{:S(2)}) %collective-permute-start) | collective-permute-done | bytes 524320 | tf_op jit(solution)/shard_map/cond/branch_1_fun/ppermute | solution.py:19
  30.9 4.9 %branch_1_fun.4 = bf16[4,256,256]{2,1,0:T(8,128)(2,1)S(1)} custom-call(s32[3]{0:T(128)S(1)} %get-tuple-element.51.refs_0_, s32[3,8,8]{2,1,0:T(8,128)S(1)} %get-tuple-element.52.refs_1_, bf16[4,256,256]{2,1,0:T(8,128)(2,1)S(1)} %get-tuple-element.53.refs_2_, bf16[4,256,256]{2,1,0:T(8,128)(2,1)S(1)} %collective-permute-done.refs_3_, ...), custom_call_target="tpu_custom_call" | custom-call | flops 1 | bytes 1 | tf_op jit(solution)/shard_map/cond/branch_1_fun/pallas_call | solution.py:369
  35.8 3.0 %collective-permute-done.10 = bf16[1168,256]{1,0:T(8,128)(2,1)} collective-permute-done((bf16[1168,256]{1,0:T(8,128)(2,1)}, bf16[1168,256]{1,0:T(8,128)(2,1)}, u32[]{:S(2)}, u32[]{:S(2)}) %collective-permute-start.10) | collective-permute-done | bytes 598048 | tf_op jit(solution)/shard_map/ppermute | solution.py:24
  38.8 12.7 %conditional.5 = (bf16[2,256,256]{2,1,0:T(8,128)(2,1)S(1)}) conditional(s32[]{:T(128)} %bitcast, () %tuple.24, (bf16[4,256,256]{2,1,0:T(8,128)(2,1)S(1)}, bf16[1168,256]{1,0:T(8,128)(2,1)}, bf16[1168,256]{1,0:T(8,128)(2,1)}, s32[3]{0:T(128)S(1)}, s32[3,8,8]{2,1,0:T(8,128)S(1)}, /*index=5*/f32[8,256,128]{2,1,0:T(8,128)S(1)}) %tuple.42), branch_computations={%region_4.0_spmd, %region_5.0_spmd} | conditional | flops 1 | bytes 6881409 | solution.py:399
  38.8 0.5 collective-permute-start.4
  39.3 0.0 collective-permute-start.2
  39.3 3.0 %collective-permute-done.2.refs_3_ = bf16[4,256,256]{2,1,0:T(8,128)(2,1)S(1)} collective-permute-done((bf16[4,256,256]{2,1,0:T(8,128)(2,1)S(1)}, bf16[4,256,256]{2,1,0:T(8,128)(2,1)S(1)}, u32[]{:S(2)}, u32[]{:S(2)}) %collective-permute-start.2) | collective-permute-done | bytes 524320 | tf_op jit(solution)/shard_map/cond/branch_1_fun/ppermute | solution.py:19
  42.3 0.3 collective-permute-done.4.refs_8_
  42.6 8.9 %branch_1_fun.5 = bf16[2,256,256]{2,1,0:T(8,128)(2,1)S(1)} custom-call(s32[3]{0:T(128)S(1)} %get-tuple-element.56.refs_0_, s32[3,8,8]{2,1,0:T(8,128)S(1)} %get-tuple-element.57.refs_1_, bf16[4,256,256]{2,1,0:T(8,128)(2,1)S(1)} %get-tuple-element.58.refs_2_, bf16[4,256,256]{2,1,0:T(8,128)(2,1)S(1)} %collective-permute-done.2.refs_3_, ...), custom_call_target="tpu_custom_call" | custom-call | flops 1 | bytes 1 | tf_op jit(solution)/shard_map/cond/branch_1_fun/pallas_call | solution.py:344
  51.5 1.4 %collective-permute-start.12 = (bf16[256,256]{1,0:T(8,128)(2,1)S(1)}, bf16[256,256]{1,0:T(8,128)(2,1)S(1)}, u32[]{:S(2)}, u32[]{:S(2)}) collective-permute-start(bf16[256,256]{1,0:T(8,128)(2,1)S(1)} %get-tuple-element.73), channel_id=1, source_target_pairs={{0,2},{1,3},{2,0},{3,1},{4,6},{5,7},{6,4},{7,5},{8,10},{9,11},{10,... | collective-permute-start | bytes 393224 | tf_op jit(solution)/shard_map/ppermute | solution.py:19
  53.0 4.1 %collective-permute-done.12 = bf16[256,256]{1,0:T(8,128)(2,1)S(1)} collective-permute-done((bf16[256,256]{1,0:T(8,128)(2,1)S(1)}, bf16[256,256]{1,0:T(8,128)(2,1)S(1)}, u32[]{:S(2)}, u32[]{:S(2)}) %collective-permute-start.12) | collective-permute-done | bytes 131104 | tf_op jit(solution)/shard_map/ppermute | solution.py:19
  57.1 0.7 %maximum_select_fusion = bf16[2,1,16,16,256]{4,3,2,1,0:T(8,128)(2,1)} fusion(bf16[1,1,16,16,256]{4,3,2,1,0:T(8,128)(2,1)S(1)} %bitcast.23, bf16[1,1,16,16,256]{4,3,2,1,0:T(8,128)(2,1)S(1)} %bitcast.17, pred[]{:T(512)S(6)} %eq.3), kind=kLoop, calls=%fused_computation.1 | loop fusion | flops 393216 | bytes 524289 | tf_op jit(solution)/shard_map/jit(_where)/select_n | solution.py:426
  (11 shorter events, 0.0 us)
Async XLA Ops:
  0.1 21.2 %copy-start.1 = (s32[3,8,8]{2,1,0:T(8,128)S(1)}, s32[3,8,8]{2,1,0:T(8,128)}, u32[]{:S(2)}) copy-start(s32[3,8,8]{2,1,0:T(8,128)} %param.17) | copy-start | bytes 2308
  0.1 23.1 %copy-start = (bf16[1,9,256,256]{3,2,1,0:T(8,128)(2,1)S(1)}, bf16[1,9,256,256]{3,2,1,0:T(8,128)(2,1)}, u32[]{:S(2)}) copy-start(bf16[1,9,256,256]{3,2,1,0:T(8,128)(2,1)} %param.13) | copy-start | bytes 3538948
  3.1 9.9 %collective-permute-start.7 = (bf16[272,256]{1,0:T(8,128)(2,1)}, bf16[272,256]{1,0:T(8,128)(2,1)S(1)}, u32[]{:S(2)}, u32[]{:S(2)}) collective-permute-start(bf16[272,256]{1,0:T(8,128)(2,1)} %get-tuple-element.69), channel_id=1, source_target_pairs={{0,6},{1,7},{2,4},{3,5},{4,2},{5,3},{6,0},{7,1},{8,14},{9,15},{10,... | collective-permute-start | bytes 417800 | tf_op jit(solution)/shard_map/ppermute | solution.py:19
  8.2 8.0 %collective-permute-start.5 = (bf16[272,256]{1,0:T(8,128)(2,1)}, bf16[272,256]{1,0:T(8,128)(2,1)S(1)}, u32[]{:S(2)}, u32[]{:S(2)}) collective-permute-start(bf16[272,256]{1,0:T(8,128)(2,1)} %get-tuple-element.69), channel_id=1, source_target_pairs={{0,2},{1,3},{2,0},{3,1},{4,6},{5,7},{6,4},{7,5},{8,10},{9,11},{10,... | collective-permute-start | bytes 417800 | tf_op jit(solution)/shard_map/ppermute | solution.py:19
  8.2 12.0 %collective-permute-start.6 = (bf16[272,256]{1,0:T(8,128)(2,1)}, bf16[272,256]{1,0:T(8,128)(2,1)S(1)}, u32[]{:S(2)}, u32[]{:S(2)}) collective-permute-start(bf16[272,256]{1,0:T(8,128)(2,1)} %get-tuple-element.68), channel_id=1, source_target_pairs={{0,4},{1,5},{2,6},{3,7},{4,0},{5,1},{6,2},{7,3},{8,12},{9,13},{10,... | collective-permute-start | bytes 417800 | tf_op jit(solution)/shard_map/ppermute | solution.py:19
  8.8 19.2 %collective-permute-start.9 = (bf16[1168,256]{1,0:T(8,128)(2,1)}, bf16[1168,256]{1,0:T(8,128)(2,1)}, u32[]{:S(2)}, u32[]{:S(2)}) collective-permute-start(bf16[1168,256]{1,0:T(8,128)(2,1)} %get-tuple-element.67), channel_id=1, source_target_pairs={{8,0},{16,8},{24,16},{0,24},{9,1},{17,9},{25,17},{1,25},{10,2},{18... | collective-permute-start | bytes 1794056 | tf_op jit(solution)/shard_map/ppermute | solution.py:24
  11.4 27.4 %collective-permute-start.10 = (bf16[1168,256]{1,0:T(8,128)(2,1)}, bf16[1168,256]{1,0:T(8,128)(2,1)}, u32[]{:S(2)}, u32[]{:S(2)}) collective-permute-start(bf16[1168,256]{1,0:T(8,128)(2,1)} %get-tuple-element.67), channel_id=1, source_target_pairs={{16,0},{24,8},{0,16},{8,24},{17,1},{25,9},{1,17},{9,25},{18,2},{26... | collective-permute-start | bytes 1794056 | tf_op jit(solution)/shard_map/ppermute | solution.py:24
  12.9 25.9 %collective-permute-start.11 = (bf16[1168,256]{1,0:T(8,128)(2,1)}, bf16[1168,256]{1,0:T(8,128)(2,1)}, u32[]{:S(2)}, u32[]{:S(2)}) collective-permute-start(bf16[1168,256]{1,0:T(8,128)(2,1)} %get-tuple-element.67), channel_id=1, source_target_pairs={{24,0},{0,8},{8,16},{16,24},{25,1},{1,9},{9,17},{17,25},{26,2},{2,... | collective-permute-start | bytes 1794056 | tf_op jit(solution)/shard_map/ppermute | solution.py:24
  21.1 2.0 %collective-permute-start.8 = (bf16[4,272,256]{2,1,0:T(8,128)(2,1)S(1)}, bf16[4,272,256]{2,1,0:T(8,128)(2,1)S(1)}, u32[]{:S(2)}, u32[]{:S(2)}) collective-permute-start(bf16[4,272,256]{2,1,0:T(8,128)(2,1)S(1)} %pad_maximum_fusion), channel_id=1, source_target_pairs={{0,1},{1,0},{2,3},{3,2},{4,5},{5,4},{6,7},{7,6},{8,9},{9,8},{10,11... | collective-permute-start | bytes 1671176 | tf_op jit(solution)/shard_map/ppermute | solution.py:19
  28.1 2.8 %collective-permute-start.1 = (bf16[1168,256]{1,0:T(8,128)(2,1)}, bf16[1168,256]{1,0:T(8,128)(2,1)S(1)}, u32[]{:S(2)}, u32[]{:S(2)}) collective-permute-start(bf16[1168,256]{1,0:T(8,128)(2,1)} %get-tuple-element.55.refs_5_), channel_id=1, source_target_pairs={{0,1},{1,0},{2,3},{3,2},{4,5},{5,4},{6,7},{7,6},{8,9},{9,8},{10,11... | collective-permute-start | bytes 1794056 | tf_op jit(solution)/shard_map/cond/branch_1_fun/ppermute | solution.py:19
  28.3 2.6 %collective-permute-start = (bf16[4,256,256]{2,1,0:T(8,128)(2,1)S(1)}, bf16[4,256,256]{2,1,0:T(8,128)(2,1)S(1)}, u32[]{:S(2)}, u32[]{:S(2)}) collective-permute-start(bf16[4,256,256]{2,1,0:T(8,128)(2,1)S(1)} %get-tuple-element.53.refs_2_), channel_id=1, source_target_pairs={{0,1},{1,0},{2,3},{3,2},{4,5},{5,4},{6,7},{7,6},{8,9},{9,8},{10,11... | collective-permute-start | bytes 1572872 | tf_op jit(solution)/shard_map/cond/branch_1_fun/ppermute | solution.py:19
  38.8 3.5 %collective-permute-start.3 = (bf16[1168,256]{1,0:T(8,128)(2,1)}, bf16[1168,256]{1,0:T(8,128)(2,1)S(1)}, u32[]{:S(2)}, u32[]{:S(2)}) collective-permute-start(bf16[1168,256]{1,0:T(8,128)(2,1)} %get-tuple-element.60.refs_5_), channel_id=1, source_target_pairs={{0,1},{1,0},{2,3},{3,2},{4,5},{5,4},{6,7},{7,6},{8,9},{9,8},{10,11... | collective-permute-start | bytes 1794056 | tf_op jit(solution)/shard_map/cond/branch_1_fun/ppermute | solution.py:19
  38.8 3.8 %collective-permute-start.4 = (bf16[1168,256]{1,0:T(8,128)(2,1)}, bf16[1168,256]{1,0:T(8,128)(2,1)S(1)}, u32[]{:S(2)}, u32[]{:S(2)}) collective-permute-start(bf16[1168,256]{1,0:T(8,128)(2,1)} %get-tuple-element.61.refs_7_), channel_id=1, source_target_pairs={{0,1},{1,0},{2,3},{3,2},{4,5},{5,4},{6,7},{7,6},{8,9},{9,8},{10,11... | collective-permute-start | bytes 1794056 | tf_op jit(solution)/shard_map/cond/branch_1_fun/ppermute | solution.py:19
  39.3 3.0 %collective-permute-start.2 = (bf16[4,256,256]{2,1,0:T(8,128)(2,1)S(1)}, bf16[4,256,256]{2,1,0:T(8,128)(2,1)S(1)}, u32[]{:S(2)}, u32[]{:S(2)}) collective-permute-start(bf16[4,256,256]{2,1,0:T(8,128)(2,1)S(1)} %get-tuple-element.58.refs_2_), channel_id=1, source_target_pairs={{0,1},{1,0},{2,3},{3,2},{4,5},{5,4},{6,7},{7,6},{8,9},{9,8},{10,11... | collective-permute-start | bytes 1572872 | tf_op jit(solution)/shard_map/cond/branch_1_fun/ppermute | solution.py:19
  51.5 5.6 %collective-permute-start.12 = (bf16[256,256]{1,0:T(8,128)(2,1)S(1)}, bf16[256,256]{1,0:T(8,128)(2,1)S(1)}, u32[]{:S(2)}, u32[]{:S(2)}) collective-permute-start(bf16[256,256]{1,0:T(8,128)(2,1)S(1)} %get-tuple-element.73), channel_id=1, source_target_pairs={{0,2},{1,3},{2,0},{3,1},{4,6},{5,7},{6,4},{7,5},{8,10},{9,11},{10,... | collective-permute-start | bytes 393224 | tf_op jit(solution)/shard_map/ppermute | solution.py:19

commit v3 on v2

--- a/solution.py
+++ b/solution.py
@@ -110,7 +110,7 @@
         def _(j):
             for ref, b in ((even, 2 * j), (odd, 2 * j + 1)):
                 normed_tile(b, lambda part: ref[j, part].astype(F32))
-                mt[b, :, 0:EXTRA] = jnp.transpose(ref[j, px : px + EXTRA, :].astype(F32))
+                mt[b, 0:px, 0:EXTRA] = jnp.transpose(ref[j, px : px + EXTRA, :].astype(F32))
 
     elif source == "full":
 
@@ -189,7 +189,7 @@
         frames(b)
         for at in range(-1, side + 1):
             spread_line(place, at + 1, b, "row", at)
-        metric = mt[b]
+        metric = mt[b, 0:px]
         for q in range(9):
             a, c = q // 3, q % 3
             taps = jnp.broadcast_to(metric[:, q : q + 1], (px, LANES)).astype(BF16)
@@ -312,8 +312,8 @@
     lines = 4 * depth_out if depth_out else 1
     line_rows = lines * side * (tiles - 2) if depth_out else 2 * side
     return [
-        pltpu.VMEM((tiles, halves, px, LANES), F32),
-        pltpu.VMEM((halves, px, LANES), F32),
+        pltpu.VMEM((tiles, halves, px + side, LANES), F32),
+        pltpu.VMEM((halves, px + side, LANES), F32),
         pltpu.VMEM((tiles, lines, side, ch), BF16),
         pltpu.VMEM((4, halves, side, LANES), F32),
         pltpu.VMEM((4, halves, 1, LANES), F32),
@@ -360,7 +360,7 @@
     if depth_out is None:
         shapes = [jax.ShapeDtypeStruct((tiles // 2, px, ch), BF16)]
         if not copied:
-            shapes.append(jax.ShapeDtypeStruct((tiles, px, LANES), F32))
+            shapes.append(jax.ShapeDtypeStruct((tiles, px + side, LANES), F32))
     else:
         shapes = [jax.ShapeDtypeStruct((2, px, ch), BF16)]
         if depth_out:

time: 58.1 us -> 58.1 us (level)
  no operation moved by 1% of the time
where the time goes in v3:
time: 58.1 us; the launch traced here: 57.8 us
  Pallas kernels  20.9 us (36%)
  waiting for transfers between devices  20 us (34%)
  starting transfers between devices  13.2 us (23%)
  other arithmetic  1.78 us (3%)
  local copies, waits for them, and re-layouts  1.24 us (2%)
  between operations  0.73 us (1%)
    ppermute x10, waiting for transfers between devices, swap(): return lax.ppermute(value, axis, [(i, i ^ by) for i in range(peers)])  17 us
    pallas_call x2, Pallas kernels, layer(): pl.pallas_call(functools.partial(layer_kernel, side, tiles, source, depth...  9.05 us
    pallas_call x1, Pallas kernels, last_layers(): pl.pallas_call(functools.partial(last_layers_kernel, side, tiles), out_sh...  8.83 us
    ppermute x10, starting transfers between devices, swap(): return lax.ppermute(value, axis, [(i, i ^ by) for i in range(peers)])  8.37 us
    ppermute x3, starting transfers between devices, fetch(): lax.ppermute(value, axis, [((i + by) % peers, i) for i in range(peers)])  4.79 us
    ppermute x3, waiting for transfers between devices, fetch(): lax.ppermute(value, axis, [((i + by) % peers, i) for i in range(peers)])  3 us
    pallas_call x1, Pallas kernels, pack(): pl.pallas_call(pack_kernel, out_shape=(state, state, half), in_specs=[SME...  2.97 us
  transfers between devices with their start and end apart: 13, of which 9 were waited for; matrix products, arithmetic and copies ran while one was open for 4% of the time, Pallas kernels for 16%

profile of v3, /device:TPU:0, one launch (start us, length us, event | category | flops | bytes accessed | tf_op | source)
XLA Modules:
  0.0 57.8 jit_solution(16607174585449945667)
XLA Ops:
  0.0 0.1 pad_add_fusion.ids
  0.1 3.0 %shard_map.64 = (bf16[272,256]{1,0:T(8,128)(2,1)}, bf16[272,256]{1,0:T(8,128)(2,1)}, bf16[1168,256]{1,0:T(8,128)(2,1)}) custom-call(s32[3]{0:T(128)S(1)} %pad_add_fusion.ids, bf16[2,256,256]{2,1,0:T(8,128)(2,1)} %bitcast.18, bf16[9,256]{1,0:T(8,128)(2,1)} %bitcast.24, bf16[2304,256]{1,0:T(8,128)(2,1)} %bitcast.15, bf16[1,256]{1,0:T(2,128)(2,1)} %gain.1, ...), custom_call_target="tpu_custom_call" | custom-call | tf_op jit(solution)/shard_map/pallas_call | solution.py:284
  3.1 5.1 %collective-permute-start.7 = (bf16[272,256]{1,0:T(8,128)(2,1)}, bf16[272,256]{1,0:T(8,128)(2,1)S(1)}, u32[]{:S(2)}, u32[]{:S(2)}) collective-permute-start(bf16[272,256]{1,0:T(8,128)(2,1)} %get-tuple-element.69), channel_id=1, source_target_pairs={{0,6},{1,7},{2,4},{3,5},{4,2},{5,3},{6,0},{7,1},{8,14},{9,15},{10,... | collective-permute-start | bytes 417800 | tf_op jit(solution)/shard_map/ppermute | solution.py:19
  8.2 0.6 %collective-permute-start.6 = (bf16[272,256]{1,0:T(8,128)(2,1)}, bf16[272,256]{1,0:T(8,128)(2,1)S(1)}, u32[]{:S(2)}, u32[]{:S(2)}) collective-permute-start(bf16[272,256]{1,0:T(8,128)(2,1)} %get-tuple-element.68), channel_id=1, source_target_pairs={{0,4},{1,5},{2,6},{3,7},{4,0},{5,1},{6,2},{7,3},{8,12},{9,13},{10,... | collective-permute-start | bytes 417800 | tf_op jit(solution)/shard_map/ppermute | solution.py:19
  8.8 2.6 %collective-permute-start.9 = (bf16[1168,256]{1,0:T(8,128)(2,1)}, bf16[1168,256]{1,0:T(8,128)(2,1)}, u32[]{:S(2)}, u32[]{:S(2)}) collective-permute-start(bf16[1168,256]{1,0:T(8,128)(2,1)} %get-tuple-element.67), channel_id=1, source_target_pairs={{8,0},{16,8},{24,16},{0,24},{9,1},{17,9},{25,17},{1,25},{10,2},{18... | collective-permute-start | bytes 1794056 | tf_op jit(solution)/shard_map/ppermute | solution.py:24
  11.4 0.5 collective-permute-start.10
  11.9 1.0 %collective-permute-done.7 = bf16[272,256]{1,0:T(8,128)(2,1)S(1)} collective-permute-done((bf16[272,256]{1,0:T(8,128)(2,1)}, bf16[272,256]{1,0:T(8,128)(2,1)S(1)}, u32[]{:S(2)}, u32[]{:S(2)}) %collective-permute-start.7) | collective-permute-done | bytes 139296 | tf_op jit(solution)/shard_map/ppermute | solution.py:19
  12.9 1.7 %collective-permute-start.11 = (bf16[1168,256]{1,0:T(8,128)(2,1)}, bf16[1168,256]{1,0:T(8,128)(2,1)}, u32[]{:S(2)}, u32[]{:S(2)}) collective-permute-start(bf16[1168,256]{1,0:T(8,128)(2,1)} %get-tuple-element.67), channel_id=1, source_target_pairs={{24,0},{0,8},{8,16},{16,24},{25,1},{1,9},{9,17},{17,25},{26,2},{2,... | collective-permute-start | bytes 1794056 | tf_op jit(solution)/shard_map/ppermute | solution.py:24
  14.6 1.5 %collective-permute-done.5 = bf16[272,256]{1,0:T(8,128)(2,1)S(1)} collective-permute-done((bf16[272,256]{1,0:T(8,128)(2,1)}, bf16[272,256]{1,0:T(8,128)(2,1)S(1)}, u32[]{:S(2)}, u32[]{:S(2)}) %collective-permute-start.5) | collective-permute-done | bytes 139296 | tf_op jit(solution)/shard_map/ppermute | solution.py:19
  16.1 4.0 %collective-permute-done.6 = bf16[272,256]{1,0:T(8,128)(2,1)S(1)} collective-permute-done((bf16[272,256]{1,0:T(8,128)(2,1)}, bf16[272,256]{1,0:T(8,128)(2,1)S(1)}, u32[]{:S(2)}, u32[]{:S(2)}) %collective-permute-start.6) | collective-permute-done | bytes 139296 | tf_op jit(solution)/shard_map/ppermute | solution.py:19
  20.2 1.0 %pad_maximum_fusion = bf16[4,272,256]{2,1,0:T(8,128)(2,1)S(1)} fusion(bf16[1,272,256]{2,1,0:T(8,128)(2,1)S(1)} %bitcast.20, bf16[1,272,256]{2,1,0:T(8,128)(2,1)S(1)} %bitcast.22, bf16[1,272,256]{2,1,0:T(8,128)(2,1)S(1)} %bitcast.21, bf16[1,272,256]{2,1,0:T(8,128)(2,1)} %bitcast.19), kind=kLoop, calls=%fused_computation | loop fusion | flops 835584 | bytes 1114112 | tf_op jit(solution)/shard_map/stack | solution.py:404
  21.1 0.1 collective-permute-start.8
  21.2 0.5 slice.13
  22.4 0.8 %collective-permute-done.8 = bf16[4,272,256]{2,1,0:T(8,128)(2,1)S(1)} collective-permute-done((bf16[4,272,256]{2,1,0:T(8,128)(2,1)S(1)}, bf16[4,272,256]{2,1,0:T(8,128)(2,1)S(1)}, u32[]{:S(2)}, u32[]{:S(2)}) %collective-permute-start.8) | collective-permute-done | bytes 557088 | tf_op jit(solution)/shard_map/ppermute | solution.py:19
  23.2 4.8 %conditional.3 = ((bf16[4,256,256]{2,1,0:T(8,128)(2,1)S(1)}, f32[8,272,128]{2,1,0:T(8,128)S(1)})) conditional(s32[]{:T(128)} %bitcast, () %tuple.26, (bf16[1168,256]{1,0:T(8,128)(2,1)}, s32[3]{0:T(128)S(1)}, s32[3,8,8]{2,1,0:T(8,128)S(1)}, bf16[4,272,256]{2,1,0:T(8,128)(2,1)S(1)}, bf16[4,272,256]{2,1,0:T(8,128)(2,1)S(1)}, ...), branch_computations={%region_0.0_spmd, %region_1.0_spmd} | conditional | flops 1 | bytes 1638430 | solution.py:399
  23.2 0.7 %slice.4.refs_5_ = bf16[16,256]{1,0:T(8,128)(2,1)S(1)} slice(bf16[1168,256]{1,0:T(8,128)(2,1)} %get-tuple-element.50), slice={[1152:1168], [0:256]} | slice | bytes 16384 | tf_op jit(solution)/shard_map/cond/branch_1_fun/slice | solution.py:408
  23.9 4.1 %branch_1_fun.3 = (bf16[4,256,256]{2,1,0:T(8,128)(2,1)S(1)}, f32[8,272,128]{2,1,0:T(8,128)S(1)}) custom-call(s32[3]{0:T(128)S(1)} %get-tuple-element.44.refs_0_, s32[3,8,8]{2,1,0:T(8,128)S(1)} %get-tuple-element.46.refs_1_, bf16[4,272,256]{2,1,0:T(8,128)(2,1)S(1)} %get-tuple-element.47.refs_2_, bf16[4,272,256]{2,1,0:T(8,128)(2,1)S(1)} %get-tuple-element.48.refs_3_, ...), custom_call_target="tpu_custom_call" | custom-call | flops 1 | bytes 1 | tf_op jit(solution)/shard_map/cond/branch_1_fun/pallas_call | solution.py:369
  28.0 7.8 %conditional.4 = (bf16[4,256,256]{2,1,0:T(8,128)(2,1)S(1)}) conditional(s32[]{:T(128)} %bitcast, () %tuple.25, (bf16[4,256,256]{2,1,0:T(8,128)(2,1)S(1)}, bf16[1168,256]{1,0:T(8,128)(2,1)}, s32[3]{0:T(128)S(1)}, s32[3,8,8]{2,1,0:T(8,128)S(1)}, f32[8,272,128]{2,1,0:T(8,128)S(1)}) %tuple.41), branch_computations={%region_2.0_spmd, %region_3.0_spmd} | conditional | flops 1 | bytes 4489305 | solution.py:399
  28.0 0.2 collective-permute-start.1
  28.3 0.4 collective-permute-start
  28.6 2.3 %collective-permute-done.refs_3_ = bf16[4,256,256]{2,1,0:T(8,128)(2,1)S(1)} collective-permute-done((bf16[4,256,256]{2,1,0:T(8,128)(2,1)S(1)}, bf16[4,256,256]{2,1,0:T(8,128)(2,1)S(1)}, u32[]{:S(2)}, u32[]{:S(2)}) %collective-permute-start) | collective-permute-done | bytes 524320 | tf_op jit(solution)/shard_map/cond/branch_1_fun/ppermute | solution.py:19
  30.9 4.9 %branch_1_fun.4 = bf16[4,256,256]{2,1,0:T(8,128)(2,1)S(1)} custom-call(s32[3]{0:T(128)S(1)} %get-tuple-element.51.refs_0_, s32[3,8,8]{2,1,0:T(8,128)S(1)} %get-tuple-element.52.refs_1_, bf16[4,256,256]{2,1,0:T(8,128)(2,1)S(1)} %get-tuple-element.53.refs_2_, bf16[4,256,256]{2,1,0:T(8,128)(2,1)S(1)} %collective-permute-done.refs_3_, ...), custom_call_target="tpu_custom_call" | custom-call | flops 1 | bytes 1 | tf_op jit(solution)/shard_map/cond/branch_1_fun/pallas_call | solution.py:369
  35.8 3.0 %collective-permute-done.10 = bf16[1168,256]{1,0:T(8,128)(2,1)} collective-permute-done((bf16[1168,256]{1,0:T(8,128)(2,1)}, bf16[1168,256]{1,0:T(8,128)(2,1)}, u32[]{:S(2)}, u32[]{:S(2)}) %collective-permute-start.10) | collective-permute-done | bytes 598048 | tf_op jit(solution)/shard_map/ppermute | solution.py:24
  38.8 12.7 %conditional.5 = (bf16[2,256,256]{2,1,0:T(8,128)(2,1)S(1)}) conditional(s32[]{:T(128)} %bitcast, () %tuple.24, (bf16[4,256,256]{2,1,0:T(8,128)(2,1)S(1)}, bf16[1168,256]{1,0:T(8,128)(2,1)}, bf16[1168,256]{1,0:T(8,128)(2,1)}, s32[3]{0:T(128)S(1)}, s32[3,8,8]{2,1,0:T(8,128)S(1)}, /*index=5*/f32[8,272,128]{2,1,0:T(8,128)S(1)}) %tuple.42), branch_computations={%region_4.0_spmd, %region_5.0_spmd} | conditional | flops 1 | bytes 6881409 | solution.py:399
  38.8 0.5 collective-permute-start.4
  39.3 0.0 collective-permute-start.2
  39.3 3.0 %collective-permute-done.2.refs_3_ = bf16[4,256,256]{2,1,0:T(8,128)(2,1)S(1)} collective-permute-done((bf16[4,256,256]{2,1,0:T(8,128)(2,1)S(1)}, bf16[4,256,256]{2,1,0:T(8,128)(2,1)S(1)}, u32[]{:S(2)}, u32[]{:S(2)}) %collective-permute-start.2) | collective-permute-done | bytes 524320 | tf_op jit(solution)/shard_map/cond/branch_1_fun/ppermute | solution.py:19
  42.3 0.3 collective-permute-done.4.refs_8_
  42.6 8.8 %branch_1_fun.5 = bf16[2,256,256]{2,1,0:T(8,128)(2,1)S(1)} custom-call(s32[3]{0:T(128)S(1)} %get-tuple-element.56.refs_0_, s32[3,8,8]{2,1,0:T(8,128)S(1)} %get-tuple-element.57.refs_1_, bf16[4,256,256]{2,1,0:T(8,128)(2,1)S(1)} %get-tuple-element.58.refs_2_, bf16[4,256,256]{2,1,0:T(8,128)(2,1)S(1)} %collective-permute-done.2.refs_3_, ...), custom_call_target="tpu_custom_call" | custom-call | flops 1 | bytes 1 | tf_op jit(solution)/shard_map/cond/branch_1_fun/pallas_call | solution.py:344
  51.5 1.4 %collective-permute-start.12 = (bf16[256,256]{1,0:T(8,128)(2,1)S(1)}, bf16[256,256]{1,0:T(8,128)(2,1)S(1)}, u32[]{:S(2)}, u32[]{:S(2)}) collective-permute-start(bf16[256,256]{1,0:T(8,128)(2,1)S(1)} %get-tuple-element.73), channel_id=1, source_target_pairs={{0,2},{1,3},{2,0},{3,1},{4,6},{5,7},{6,4},{7,5},{8,10},{9,11},{10,... | collective-permute-start | bytes 393224 | tf_op jit(solution)/shard_map/ppermute | solution.py:19
  53.0 4.1 %collective-permute-done.12 = bf16[256,256]{1,0:T(8,128)(2,1)S(1)} collective-permute-done((bf16[256,256]{1,0:T(8,128)(2,1)S(1)}, bf16[256,256]{1,0:T(8,128)(2,1)S(1)}, u32[]{:S(2)}, u32[]{:S(2)}) %collective-permute-start.12) | collective-permute-done | bytes 131104 | tf_op jit(solution)/shard_map/ppermute | solution.py:19
  57.1 0.7 %maximum_select_fusion = bf16[2,1,16,16,256]{4,3,2,1,0:T(8,128)(2,1)} fusion(bf16[1,1,16,16,256]{4,3,2,1,0:T(8,128)(2,1)S(1)} %bitcast.23, bf16[1,1,16,16,256]{4,3,2,1,0:T(8,128)(2,1)S(1)} %bitcast.17, pred[]{:T(512)S(6)} %eq.3), kind=kLoop, calls=%fused_computation.1 | loop fusion | flops 393216 | bytes 524289 | tf_op jit(solution)/shard_map/jit(_where)/select_n | solution.py:426
  (11 shorter events, 0.0 us)
Async XLA Ops:
  0.1 21.2 %copy-start.1 = (s32[3,8,8]{2,1,0:T(8,128)S(1)}, s32[3,8,8]{2,1,0:T(8,128)}, u32[]{:S(2)}) copy-start(s32[3,8,8]{2,1,0:T(8,128)} %param.17) | copy-start | bytes 2308
  0.1 23.1 %copy-start = (bf16[1,9,256,256]{3,2,1,0:T(8,128)(2,1)S(1)}, bf16[1,9,256,256]{3,2,1,0:T(8,128)(2,1)}, u32[]{:S(2)}) copy-start(bf16[1,9,256,256]{3,2,1,0:T(8,128)(2,1)} %param.13) | copy-start | bytes 3538948
  3.1 9.9 %collective-permute-start.7 = (bf16[272,256]{1,0:T(8,128)(2,1)}, bf16[272,256]{1,0:T(8,128)(2,1)S(1)}, u32[]{:S(2)}, u32[]{:S(2)}) collective-permute-start(bf16[272,256]{1,0:T(8,128)(2,1)} %get-tuple-element.69), channel_id=1, source_target_pairs={{0,6},{1,7},{2,4},{3,5},{4,2},{5,3},{6,0},{7,1},{8,14},{9,15},{10,... | collective-permute-start | bytes 417800 | tf_op jit(solution)/shard_map/ppermute | solution.py:19
  8.2 8.0 %collective-permute-start.5 = (bf16[272,256]{1,0:T(8,128)(2,1)}, bf16[272,256]{1,0:T(8,128)(2,1)S(1)}, u32[]{:S(2)}, u32[]{:S(2)}) collective-permute-start(bf16[272,256]{1,0:T(8,128)(2,1)} %get-tuple-element.69), channel_id=1, source_target_pairs={{0,2},{1,3},{2,0},{3,1},{4,6},{5,7},{6,4},{7,5},{8,10},{9,11},{10,... | collective-permute-start | bytes 417800 | tf_op jit(solution)/shard_map/ppermute | solution.py:19
  8.2 12.0 %collective-permute-start.6 = (bf16[272,256]{1,0:T(8,128)(2,1)}, bf16[272,256]{1,0:T(8,128)(2,1)S(1)}, u32[]{:S(2)}, u32[]{:S(2)}) collective-permute-start(bf16[272,256]{1,0:T(8,128)(2,1)} %get-tuple-element.68), channel_id=1, source_target_pairs={{0,4},{1,5},{2,6},{3,7},{4,0},{5,1},{6,2},{7,3},{8,12},{9,13},{10,... | collective-permute-start | bytes 417800 | tf_op jit(solution)/shard_map/ppermute | solution.py:19
  8.8 19.2 %collective-permute-start.9 = (bf16[1168,256]{1,0:T(8,128)(2,1)}, bf16[1168,256]{1,0:T(8,128)(2,1)}, u32[]{:S(2)}, u32[]{:S(2)}) collective-permute-start(bf16[1168,256]{1,0:T(8,128)(2,1)} %get-tuple-element.67), channel_id=1, source_target_pairs={{8,0},{16,8},{24,16},{0,24},{9,1},{17,9},{25,17},{1,25},{10,2},{18... | collective-permute-start | bytes 1794056 | tf_op jit(solution)/shard_map/ppermute | solution.py:24
  11.4 27.4 %collective-permute-start.10 = (bf16[1168,256]{1,0:T(8,128)(2,1)}, bf16[1168,256]{1,0:T(8,128)(2,1)}, u32[]{:S(2)}, u32[]{:S(2)}) collective-permute-start(bf16[1168,256]{1,0:T(8,128)(2,1)} %get-tuple-element.67), channel_id=1, source_target_pairs={{16,0},{24,8},{0,16},{8,24},{17,1},{25,9},{1,17},{9,25},{18,2},{26... | collective-permute-start | bytes 1794056 | tf_op jit(solution)/shard_map/ppermute | solution.py:24
  12.9 25.9 %collective-permute-start.11 = (bf16[1168,256]{1,0:T(8,128)(2,1)}, bf16[1168,256]{1,0:T(8,128)(2,1)}, u32[]{:S(2)}, u32[]{:S(2)}) collective-permute-start(bf16[1168,256]{1,0:T(8,128)(2,1)} %get-tuple-element.67), channel_id=1, source_target_pairs={{24,0},{0,8},{8,16},{16,24},{25,1},{1,9},{9,17},{17,25},{26,2},{2,... | collective-permute-start | bytes 1794056 | tf_op jit(solution)/shard_map/ppermute | solution.py:24
  21.1 2.0 %collective-permute-start.8 = (bf16[4,272,256]{2,1,0:T(8,128)(2,1)S(1)}, bf16[4,272,256]{2,1,0:T(8,128)(2,1)S(1)}, u32[]{:S(2)}, u32[]{:S(2)}) collective-permute-start(bf16[4,272,256]{2,1,0:T(8,128)(2,1)S(1)} %pad_maximum_fusion), channel_id=1, source_target_pairs={{0,1},{1,0},{2,3},{3,2},{4,5},{5,4},{6,7},{7,6},{8,9},{9,8},{10,11... | collective-permute-start | bytes 1671176 | tf_op jit(solution)/shard_map/ppermute | solution.py:19
  28.0 2.8 %collective-permute-start.1 = (bf16[1168,256]{1,0:T(8,128)(2,1)}, bf16[1168,256]{1,0:T(8,128)(2,1)S(1)}, u32[]{:S(2)}, u32[]{:S(2)}) collective-permute-start(bf16[1168,256]{1,0:T(8,128)(2,1)} %get-tuple-element.55.refs_5_), channel_id=1, source_target_pairs={{0,1},{1,0},{2,3},{3,2},{4,5},{5,4},{6,7},{7,6},{8,9},{9,8},{10,11... | collective-permute-start | bytes 1794056 | tf_op jit(solution)/shard_map/cond/branch_1_fun/ppermute | solution.py:19
  28.3 2.6 %collective-permute-start = (bf16[4,256,256]{2,1,0:T(8,128)(2,1)S(1)}, bf16[4,256,256]{2,1,0:T(8,128)(2,1)S(1)}, u32[]{:S(2)}, u32[]{:S(2)}) collective-permute-start(bf16[4,256,256]{2,1,0:T(8,128)(2,1)S(1)} %get-tuple-element.53.refs_2_), channel_id=1, source_target_pairs={{0,1},{1,0},{2,3},{3,2},{4,5},{5,4},{6,7},{7,6},{8,9},{9,8},{10,11... | collective-permute-start | bytes 1572872 | tf_op jit(solution)/shard_map/cond/branch_1_fun/ppermute | solution.py:19
  38.8 3.5 %collective-permute-start.3 = (bf16[1168,256]{1,0:T(8,128)(2,1)}, bf16[1168,256]{1,0:T(8,128)(2,1)S(1)}, u32[]{:S(2)}, u32[]{:S(2)}) collective-permute-start(bf16[1168,256]{1,0:T(8,128)(2,1)} %get-tuple-element.60.refs_5_), channel_id=1, source_target_pairs={{0,1},{1,0},{2,3},{3,2},{4,5},{5,4},{6,7},{7,6},{8,9},{9,8},{10,11... | collective-permute-start | bytes 1794056 | tf_op jit(solution)/shard_map/cond/branch_1_fun/ppermute | solution.py:19
  38.8 3.8 %collective-permute-start.4 = (bf16[1168,256]{1,0:T(8,128)(2,1)}, bf16[1168,256]{1,0:T(8,128)(2,1)S(1)}, u32[]{:S(2)}, u32[]{:S(2)}) collective-permute-start(bf16[1168,256]{1,0:T(8,128)(2,1)} %get-tuple-element.61.refs_7_), channel_id=1, source_target_pairs={{0,1},{1,0},{2,3},{3,2},{4,5},{5,4},{6,7},{7,6},{8,9},{9,8},{10,11... | collective-permute-start | bytes 1794056 | tf_op jit(solution)/shard_map/cond/branch_1_fun/ppermute | solution.py:19
  39.3 3.0 %collective-permute-start.2 = (bf16[4,256,256]{2,1,0:T(8,128)(2,1)S(1)}, bf16[4,256,256]{2,1,0:T(8,128)(2,1)S(1)}, u32[]{:S(2)}, u32[]{:S(2)}) collective-permute-start(bf16[4,256,256]{2,1,0:T(8,128)(2,1)S(1)} %get-tuple-element.58.refs_2_), channel_id=1, source_target_pairs={{0,1},{1,0},{2,3},{3,2},{4,5},{5,4},{6,7},{7,6},{8,9},{9,8},{10,11... | collective-permute-start | bytes 1572872 | tf_op jit(solution)/shard_map/cond/branch_1_fun/ppermute | solution.py:19
  51.5 5.6 %collective-permute-start.12 = (bf16[256,256]{1,0:T(8,128)(2,1)S(1)}, bf16[256,256]{1,0:T(8,128)(2,1)S(1)}, u32[]{:S(2)}, u32[]{:S(2)}) collective-permute-start(bf16[256,256]{1,0:T(8,128)(2,1)S(1)} %get-tuple-element.73), channel_id=1, source_target_pairs={{0,2},{1,3},{2,0},{3,1},{4,6},{5,7},{6,4},{7,5},{8,10},{9,11},{10,... | collective-permute-start | bytes 393224 | tf_op jit(solution)/shard_map/ppermute | solution.py:19
